TPU v7x, 32 devices: a whole 2x2x4 slice. The times are simulated.
32 devices in a mesh: dp: 8 (over z, x), seq: 4 (over y, core).
Axes of the slice: x: 2, y: 2, z: 4, core: 2. Of those that a mesh axis runs over, the one named last changes fastest.
Arguments:
- tokens: bfloat16 [8, 8192, 768], P('dp', 'seq'), may hold values from -6 to 6
- cotangent: bfloat16 [8, 8192, 768], P('dp', 'seq'), may hold values from -6 to 6
- norm_gain: bfloat16 [768], P(('dp', 'seq')), may hold values from 0.5 to 1.5
- in_weight: bfloat16 [768, 3352], P(('dp', 'seq')), may hold values from -0.21875 to 0.21875
- conv_weight: bfloat16 [1792, 4], P(('dp', 'seq')), may hold values from -3 to 3
- conv_bias: bfloat16 [1792], P(('dp', 'seq')), may hold values from -3 to 3
- step_bias: float32 [24], replicated, may hold values from -9 to -4
- decay_log: float32 [24], replicated, may hold values from 0 to 1.5
- skip_gain: float32 [24], replicated, may hold values from 0.5 to 1.5
- gate_gain: bfloat16 [1536], P(('dp', 'seq')), may hold values from 0.5 to 1.5
- out_weight: bfloat16 [1536, 768], P(('dp', 'seq')), may hold values from -0.15625 to 0.15625
Outputs:
- mixed: bfloat16 [8, 8192, 768], P('dp', 'seq')
- tokens_grad: bfloat16 [8, 8192, 768], P('dp', 'seq')
- norm_gain_grad: float32 [768], P(('dp', 'seq'))
- in_weight_grad: float32 [768, 3352], P(('dp', 'seq'))
- conv_weight_grad: float32 [1792, 4], P(('dp', 'seq'))
- conv_bias_grad: float32 [1792], P(('dp', 'seq'))
- step_bias_grad: float32 [24], replicated
- decay_log_grad: float32 [24], replicated
- skip_gain_grad: float32 [24], replicated
- gate_gain_grad: float32 [1536], P(('dp', 'seq'))
- out_weight_grad: float32 [1536, 768], P(('dp', 'seq'))
All inputs are finite; a program needn't handle non-finite values.
Results may differ from a plain program's by a relative error of at most 0.012.
Values may be sent and summed in bfloat16 or wider, within the bound.
A program may use at most 384 MiB of HBM per device.

v0:
```python
import math

import jax
import jax.numpy as jnp
from jax import lax
from jax.sharding import PartitionSpec as P

HEADS = 24
HEADDIM = 64
NSTATE = 128
CONV = 4
BLOCK = 128
D_INNER = 1536
CHANNELS = 1792


EPSILON = 1e-05
HIGHEST = lax.Precision.HIGHEST


def from_behind(x, axis, by):
    peers = lax.axis_size(axis)
    pairs = [(i, i + by) for i in range(peers) if 0 <= i + by < peers]
    return lax.ppermute(x, axis, pairs)


def entering_2(x, axis, combine, identity, reverse):
    peers, index = (lax.axis_size(axis), lax.axis_index(axis))
    everything = jax.tree.map(
        lambda part, kind: lax.all_gather(part.astype(kind), axis), x, (jnp.bfloat16, jnp.bfloat16)
    )
    start = jax.tree.map(
        lambda part, zero: jnp.broadcast_to(jnp.asarray(zero, part.dtype), part.shape), x, identity
    )

    def step(k, before):
        at = peers - 1 - k if reverse else k
        reached = at > index if reverse else at < index
        new = combine(
            before, jax.tree.map(lambda part, own: part[at].astype(own.dtype), everything, x)
        )
        return jax.tree.map(lambda a, b: jnp.where(reached, a, b), new, before)

    return lax.fori_loop(0, peers, step, start)


def norm_input(tok_rows, gain_vec):
    inv_scale = lax.rsqrt(jnp.mean(tok_rows * tok_rows, axis=-1, keepdims=True) + EPSILON)
    return tok_rows * inv_scale * gain_vec


def conv_apply(extended, weight, bias_vec):
    seq_len = extended.shape[0] - weight.shape[1] + 1
    total_sum = bias_vec
    for offset in range(weight.shape[1]):
        total_sum = total_sum + extended[offset : offset + seq_len] * weight[:, offset]
    return jax.nn.silu(total_sum)


def make_steps(raw_steps, step_bias, decay_log):
    step_vals = jax.nn.softplus(raw_steps + step_bias)
    cumulative = jnp.cumsum(step_vals * -jnp.exp(decay_log), axis=1)
    return (step_vals, cumulative)


def causal_decay(cumulative):
    across = jnp.swapaxes(cumulative, 1, 2)
    gap_log = across[:, :, :, None] - across[:, :, None, :]
    span_len = cumulative.shape[1]
    lower_mask = lax.broadcasted_iota(jnp.int32, (span_len, span_len), 0) >= lax.broadcasted_iota(
        jnp.int32, (span_len, span_len), 1
    )
    return jnp.exp(jnp.where(lower_mask, gap_log, -jnp.inf))


def score_terms(inner_prod, step_vals, cumulative):
    return (
        inner_prod[:, None]
        * causal_decay(cumulative)
        * jnp.swapaxes(step_vals, 1, 2)[:, :, None, :]
    )


def weight_terms(values, step_vals, cumulative):
    return values * (jnp.exp(cumulative[:, -1:, :] - cumulative) * step_vals)[..., None]


def gated_norm(mixed_in, gate_in, gain_vec):
    gated = mixed_in * jax.nn.silu(gate_in)
    inv_scale = lax.rsqrt(jnp.mean(gated * gated, axis=-1, keepdims=True) + EPSILON)
    return gated * inv_scale * gain_vec


def outgoing(block_decay, states):
    inclusive = jnp.cumsum(block_decay, axis=0)
    tail_decay = jnp.exp(inclusive[-1][None, :] - inclusive)
    return jnp.einsum("dh,dhpn->hpn", tail_decay, states, precision=HIGHEST)


def state_chain(block_decay, states, incoming):
    inclusive = jnp.cumsum(block_decay, axis=0)
    exclusive = inclusive - block_decay
    gap_log = exclusive[:, None, :] - inclusive[None, :, :]
    span_len = block_decay.shape[0]
    lower_mask = lax.broadcasted_iota(jnp.int32, (span_len, span_len), 0) > lax.broadcasted_iota(
        jnp.int32, (span_len, span_len), 1
    )
    factor = jnp.exp(jnp.where(lower_mask[:, :, None], gap_log, -jnp.inf))
    within = jnp.einsum("cdh,dhpn->chpn", factor, states, precision=HIGHEST)
    entering = within + jnp.exp(exclusive)[:, :, None, None] * incoming
    leaving = outgoing(block_decay, states) + jnp.exp(inclusive[-1])[:, None, None] * incoming
    return (entering, leaving)


def combine_states(earlier, latter):
    return (earlier[0] * latter[0], earlier[1] * latter[0][:, None, None] + latter[1])


def intra_forward(pieces):
    values_g, write_g, read_g, steps_g, cum_part = pieces
    inner_prod = jnp.einsum("btn,bsn->bts", read_g, write_g, preferred_element_type=jnp.float32)
    scores = score_terms(inner_prod, steps_g, cum_part).astype(jnp.bfloat16)
    return jnp.einsum("bhts,bshp->bthp", scores, values_g, preferred_element_type=jnp.float32)


def intra_backward(pieces):
    values_g, write_g, read_g, steps_g, cum_part, upstream = pieces
    inner_prod = jnp.einsum("btn,bsn->bts", read_g, write_g, preferred_element_type=jnp.float32)
    score_pre, score_pull = jax.vjp(score_terms, inner_prod, steps_g, cum_part)
    scores = score_pre.astype(jnp.bfloat16)
    values_part = jnp.einsum(
        "bhts,bthp->bshp", scores, upstream, preferred_element_type=jnp.float32
    )
    scores_grad = jnp.einsum(
        "bthp,bshp->bhts", upstream, values_g, preferred_element_type=jnp.float32
    )
    inner_grad, step_part, cum_grad = score_pull(scores_grad)
    inner_low = inner_grad.astype(jnp.bfloat16)
    read_part = jnp.einsum("bts,bsn->btn", inner_low, write_g, preferred_element_type=jnp.float32)
    write_part = jnp.einsum("bts,btn->bsn", inner_low, read_g, preferred_element_type=jnp.float32)
    return (values_part, write_part, read_part, step_part, cum_grad)


def on_device(
    tokens,
    cotangent,
    norm_gain,
    in_weight,
    conv_weight,
    conv_bias,
    step_bias,
    decay_log,
    skip_gain,
    gate_gain,
    out_weight,
):
    gathered = (
        lax.all_gather(norm_gain, ("dp", "seq"), axis=0, tiled=True),
        lax.all_gather(in_weight, ("dp", "seq"), axis=0, tiled=True),
        lax.all_gather(conv_weight, ("dp", "seq"), axis=0, tiled=True),
        lax.all_gather(conv_bias, ("dp", "seq"), axis=0, tiled=True),
        lax.all_gather(gate_gain, ("dp", "seq"), axis=0, tiled=True),
        lax.all_gather(out_weight, ("dp", "seq"), axis=0, tiled=True),
    )
    full_norm, full_in, full_conv, full_bias, full_gate, full_out = gathered
    tok_rows = tokens[0].astype(jnp.float32)
    length = tok_rows.shape[0]
    block_count = length // BLOCK
    per_group = math.gcd(block_count, max(1, 512 // BLOCK))
    group_count = block_count // per_group

    def split_groups(block_array):
        return block_array.reshape((group_count, per_group) + block_array.shape[1:])

    def join_groups(block_array):
        return block_array.reshape((block_count,) + block_array.shape[2:])

    normed_pre, norm_pull = jax.vjp(norm_input, tok_rows, full_norm.astype(jnp.float32))
    normed = normed_pre.astype(jnp.bfloat16)
    projected = jnp.dot(normed, full_in, preferred_element_type=jnp.float32).astype(jnp.bfloat16)
    gate_rows = projected[:, :D_INNER]
    conv_in = projected[:, D_INNER : D_INNER + CHANNELS]
    raw_steps = projected[:, D_INNER + CHANNELS :]
    before = from_behind(conv_in[length - (CONV - 1) :], "seq", 1)
    extended = jnp.concatenate([before, conv_in], axis=0).astype(jnp.float32)
    activated_pre, conv_pull = jax.vjp(
        conv_apply, extended, full_conv.astype(jnp.float32), full_bias.astype(jnp.float32)
    )
    activated = activated_pre.astype(jnp.bfloat16)
    values = activated[:, :D_INNER].reshape(block_count, BLOCK, HEADS, HEADDIM)
    write_mat = activated[:, D_INNER : D_INNER + NSTATE].reshape(block_count, BLOCK, NSTATE)
    read_mat = activated[:, D_INNER + NSTATE :].reshape(block_count, BLOCK, NSTATE)
    raw_f = raw_steps.astype(jnp.float32).reshape(block_count, BLOCK, HEADS)
    (step_vals, cumulative), steps_pull = jax.vjp(make_steps, raw_f, step_bias, decay_log)
    grouped = (
        split_groups(values),
        split_groups(write_mat),
        split_groups(read_mat),
        split_groups(step_vals),
        split_groups(cumulative),
    )
    diagonal = join_groups(lax.map(intra_forward, grouped))
    values_f = values.astype(jnp.float32)
    weighted_pre, weight_pull = jax.vjp(weight_terms, values_f, step_vals, cumulative)
    weighted = weighted_pre.astype(jnp.bfloat16)
    block_states = jnp.einsum(
        "bshp,bsn->bhpn", weighted, write_mat, preferred_element_type=jnp.float32
    )
    block_decay = cumulative[:, -1, :]
    leaving_local = outgoing(block_decay, block_states)
    total_decay = jnp.exp(jnp.sum(block_decay, axis=0))
    identity = (jnp.ones_like(total_decay), jnp.zeros_like(leaving_local))
    _, incoming = entering_2((total_decay, leaving_local), "seq", combine_states, identity, False)
    chain_out, chain_pull = jax.vjp(state_chain, block_decay, block_states, incoming)
    entering = chain_out[0]
    entering_low = entering.astype(jnp.bfloat16)
    read_out = jnp.einsum(
        "btn,bhpn->bthp", read_mat, entering_low, preferred_element_type=jnp.float32
    )
    growth = jnp.exp(cumulative)[..., None]
    offdiag = growth * read_out
    mixed_sum = diagonal + offdiag + skip_gain[:, None] * values_f
    gate_f = gate_rows.astype(jnp.float32)
    normed_out_pre, gated_pull = jax.vjp(
        gated_norm, mixed_sum.reshape(length, D_INNER), gate_f, full_gate.astype(jnp.float32)
    )
    normed_out = normed_out_pre.astype(jnp.bfloat16)
    branch = jnp.dot(normed_out, full_out, preferred_element_type=jnp.float32)
    result = (tok_rows + branch).astype(jnp.bfloat16)[None]
    regathered = (
        lax.all_gather(norm_gain, ("dp", "seq"), axis=0, tiled=True),
        lax.all_gather(in_weight, ("dp", "seq"), axis=0, tiled=True),
        lax.all_gather(conv_weight, ("dp", "seq"), axis=0, tiled=True),
        lax.all_gather(conv_bias, ("dp", "seq"), axis=0, tiled=True),
        lax.all_gather(gate_gain, ("dp", "seq"), axis=0, tiled=True),
        lax.all_gather(out_weight, ("dp", "seq"), axis=0, tiled=True),
    )
    back_in = regathered[1]
    back_out = regathered[5]
    grad_seed = cotangent[0]
    out_weight_grad = lax.dot_general(
        normed_out, grad_seed, (((0,), (0,)), ((), ())), preferred_element_type=jnp.float32
    )
    normed_grad = lax.dot_general(
        grad_seed, back_out, (((1,), (1,)), ((), ())), preferred_element_type=jnp.float32
    )
    mixed_grad, gate_grad, gate_gain_grad = gated_pull(normed_grad)
    mixed_low = mixed_grad.astype(jnp.bfloat16).reshape(block_count, BLOCK, HEADS, HEADDIM)
    mixed_f = mixed_low.astype(jnp.float32)
    skip_grad = jnp.sum(mixed_f * values_f, axis=(0, 1, 3))
    read_low = (mixed_f * growth).astype(jnp.bfloat16)
    cumulative_grad = jnp.sum(mixed_f * offdiag, axis=3)
    read_grad = jnp.einsum(
        "bthp,bhpn->btn", read_low, entering_low, preferred_element_type=jnp.float32
    )
    entering_grad = jnp.einsum(
        "bthp,btn->bhpn", read_low, read_mat, preferred_element_type=jnp.float32
    )
    exclusive_growth = jnp.exp(jnp.cumsum(block_decay, axis=0) - block_decay)
    local_back = jnp.einsum("bh,bhpn->hpn", exclusive_growth, entering_grad, precision=HIGHEST)
    back_identity = (jnp.ones_like(total_decay), jnp.zeros_like(local_back))
    _, later_grad = entering_2(
        (total_decay, local_back), "seq", combine_states, back_identity, True
    )
    decay_grad, states_grad, _ = chain_pull((entering_grad, later_grad))
    cumulative_grad = cumulative_grad.at[:, -1, :].add(decay_grad)
    states_low = states_grad.astype(jnp.bfloat16)
    weighted_grad = jnp.einsum(
        "bhpn,bsn->bshp", states_low, write_mat, preferred_element_type=jnp.float32
    )
    write_grad = jnp.einsum(
        "bhpn,bshp->bsn", states_low, weighted, preferred_element_type=jnp.float32
    )
    values_weight, steps_weight, cum_weight = weight_pull(weighted_grad)
    back_groups = grouped + (split_groups(mixed_low),)
    values_part, write_part, read_part, step_part, cum_part = lax.map(intra_backward, back_groups)
    values_grad = mixed_f * skip_gain[:, None] + join_groups(values_part) + values_weight
    write_total = write_grad + join_groups(write_part)
    read_total = read_grad + join_groups(read_part)
    steps_grad = steps_weight + join_groups(step_part)
    cumulative_grad = cumulative_grad + cum_weight + join_groups(cum_part)
    raw_grad, step_bias_grad, decay_log_grad = steps_pull((steps_grad, cumulative_grad))
    activated_grad = jnp.concatenate(
        [
            values_grad.reshape(length, D_INNER),
            write_total.reshape(length, NSTATE),
            read_total.reshape(length, NSTATE),
        ],
        axis=1,
    )
    extended_grad, conv_weight_grad, conv_bias_grad = conv_pull(activated_grad)
    after_rim = from_behind(extended_grad[: CONV - 1], "seq", -1)
    conv_in_grad = extended_grad[CONV - 1 :].at[length - (CONV - 1) :].add(after_rim)
    projected_grad = jnp.concatenate(
        [gate_grad, conv_in_grad, raw_grad.reshape(length, HEADS)], axis=1
    ).astype(jnp.bfloat16)
    in_weight_grad = lax.dot_general(
        normed, projected_grad, (((0,), (0,)), ((), ())), preferred_element_type=jnp.float32
    )
    normed_in_grad = lax.dot_general(
        projected_grad, back_in, (((1,), (1,)), ((), ())), preferred_element_type=jnp.float32
    )
    rows_grad, norm_gain_grad = norm_pull(normed_in_grad)
    input_grad = (grad_seed.astype(jnp.float32) + rows_grad).astype(jnp.bfloat16)[None]
    grad_shards = (
        lax.psum_scatter(norm_gain_grad, ("dp", "seq"), scatter_dimension=0, tiled=True),
        lax.psum_scatter(in_weight_grad, ("dp", "seq"), scatter_dimension=0, tiled=True),
        lax.psum_scatter(conv_weight_grad, ("dp", "seq"), scatter_dimension=0, tiled=True),
        lax.psum_scatter(conv_bias_grad, ("dp", "seq"), scatter_dimension=0, tiled=True),
        lax.psum_scatter(gate_gain_grad, ("dp", "seq"), scatter_dimension=0, tiled=True),
        lax.psum_scatter(out_weight_grad, ("dp", "seq"), scatter_dimension=0, tiled=True),
    )
    head_sums = lax.psum((step_bias_grad, decay_log_grad, skip_grad), ("dp", "seq"))
    return (
        result,
        input_grad,
        grad_shards[0],
        grad_shards[1],
        grad_shards[2],
        grad_shards[3],
        head_sums[0],
        head_sums[1],
        head_sums[2],
        grad_shards[4],
        grad_shards[5],
    )


def solution(mesh):
    return jax.shard_map(
        on_device,
        mesh=mesh,
        in_specs=(
            P("dp", "seq", None),
            P("dp", "seq", None),
            P(("dp", "seq")),
            P(("dp", "seq"), None),
            P(("dp", "seq"), None),
            P(("dp", "seq")),
            P(),
            P(),
            P(),
            P(("dp", "seq")),
            P(("dp", "seq"), None),
        ),
        out_specs=(
            P("dp", "seq", None),
            P("dp", "seq", None),
            P(("dp", "seq")),
            P(("dp", "seq"), None),
            P(("dp", "seq"), None),
            P(("dp", "seq")),
            P(),
            P(),
            P(),
            P(("dp", "seq")),
            P(("dp", "seq"), None),
        ),
        check_vma=False,
    )
```

profile of v0, /device:TPU:0, one launch (start us, length us, event | category | flops | bytes accessed | tf_op | source)
XLA Modules:
  0.0 1101.0 jit_solution(11910852843659294130)
XLA Ops:
  10.5 42.9 %all-reduce.21 = (bf16[768]{0:T(1024)(128)(2,1)S(1)}, bf16[1792]{0:T(1024)(128)(2,1)S(1)}, bf16[1536]{0:T(1024)(128)(2,1)}) all-reduce(bf16[768]{0:T(1024)(128)(2,1)S(1)} %dynamic-update-slice.7, bf16[1792]{0:T(1024)(128)(2,1)S(1)} %dynamic-update-slice.6, ...), channel_id=1, replica_groups=mesh['dp'=8,'seq'=4] {'dp','seq'}, use_global_device_ids=true, to_apply=%add.12 | all-reduce | flops 4096 | bytes 16384
  53.4 40.7 %all-gather.3 = bf16[32,56,4]{1,2,0:T(4,128)(2,1)S(1)} all-gather(bf16[1,56,4]{1,2,0:T(4,128)(2,1)} %bitcast.399), channel_id=1, replica_groups=mesh['dp'=8,'seq'=4] {'dp','seq'}, dimensions={0}, use_global_device_ids=true | all-gather | bytes 14784 | tf_op jit(solution)/shard_map/all_gather | solution.py:160
  98.2 17.2 %convolution_convert_fusion = bf16[2048,3352]{0,1:T(8,128)(2,1)} fusion(bf16[768,3352]{1,0:T(8,128)(2,1)} %all-gather.9.cloned.1.call-done, bf16[1,2048,768]{2,1,0:T(8,128)(2,1)} %param.23, f32[768]{0:T(1024)S(1)} %convert_element_type.171, f32[2048]{0:T(1024)S(1)} %fusion.157), kind=kOutput, calls=%fused_computation.84 | convolution fusion | flops 10557636608 | bytes 22035456 | tf_op jit(solution)/shard_map/dot_general | solution.py:180
  121.5 23.3 %fusion.169 = f32[16,128,24]{2,0,1:T(8,128)S(1)} fusion(f32[16,128,24]{2,0,1:T(8,128)S(1)} %copy.320), kind=kOutput, calls=%fused_computation.265 | output fusion | flops 6242304 | bytes 393216 | tf_op jit(solution)/shard_map/jvp(jit(cumsum))/reduce_window_sum | solution.py:62
  146.2 7.4 slice.125
  153.8 12.4 %maximum_convert_fusion = f32[2051,1792]{0,1:T(8,128)} fusion(bf16[2048,1792]{0,1:T(8,128)(2,1)} %slice.125, bf16[3,1792]{0,1:T(8,128)(2,1)} %collective-permute-done), kind=kLoop, calls=%fused_computation.142 | loop fusion | flops 14701568 | bytes 22052352 | tf_op jit(solution)/shard_map/convert_element_type | solution.py:185
  166.3 34.0 %multiply_convert_fusion.8 = (bf16[2048,1792]{0,1:T(8,128)(2,1)}, f32[2048,1792]{0,1:T(8,128)}) fusion(f32[1792]{0:T(1024)S(1)} %get-tuple-element.540, f32[2051,1792]{0,1:T(8,128)} %maximum_convert_fusion, f32[1792]{0:T(1024)S(1)} %get-tuple-element.541, f32[1792]{0:T(1024)S(1)} %get-tuple-element.542, f32[1792]{0:T(1024)S(1)} %get-tuple-element.539, ...), kind=kLoop, calls=%fused_computation.92 | loop fusion | flops 47710208 | bytes 80776192 | tf_op jit(solution)/shard_map/convert_element_type | solution.py:189
  200.2 11.8 %convert_bitcast_fusion.1 = (f32[192,8,16,128]{3,1,2,0:T(8,128)}, bf16[2048,1536]{0,1:T(8,128)(2,1)}) fusion(bf16[2048,1792]{0,1:T(8,128)(2,1)} %get-tuple-element.618), kind=kLoop, calls=%fused_computation.82 | loop fusion | flops 3145728 | bytes 25165824
  214.6 12.2 %copy.424 = f32[192,8,16,128]{3,2,1,0:T(8,128)} copy(f32[192,8,16,128]{3,1,2,0:T(8,128)} %get-tuple-element.636) | data formatting | bytes 25165824
  227.4 13.2 %fusion.105 = f32[16,24,64,128]{3,2,1,0:T(8,128)} fusion(bf16[16,128,128,1]{2,1,3,0:T(8,128)(2,1)S(1)} %copy.384, f32[16,128,24,64]{1,0,3,2:T(8,128)} %bitcast.355, f32[16,128,24]{1,2,0:T(8,128)S(1)} %fusion.148), kind=kOutput, calls=%fused_computation.173 | convolution fusion | flops 811597824 | bytes 25886720 | tf_op jit(solution)/shard_map/bshp,bsn->bhpn/dot_general | solution.py:206
  240.6 18.7 %fusion.71 = f32[24,1,64,128]{3,1,2,0:T(1,128)S(1)} fusion(f32[16,24,1,1]{0,2,3,1:T(1,128)S(1)} %copy.386, f32[16,24,64,128]{3,2,1,0:T(8,128)} %fusion.105), kind=kOutput, calls=%fused_computation.137 | convolution fusion | flops 37748736 | bytes 13370880 | tf_op jit(solution)/shard_map/dh,dhpn->hpn/dot_general | solution.py:97
  274.4 11.1 %reshape_reshape.12 = bf16[4,4,128,24,64]{2,1,0,4,3:T(4,128)(2,1)} reshape(bf16[2048,1536]{0,1:T(8,128)(2,1)} %get-tuple-element.637) | data formatting | bytes 12582912 | tf_op jit(solution)/shard_map/reshape;reshape | solution.py:173
  285.5 7.2 copy.322
  299.5 20.4 %while.60 = (s32[]{:T(128)}, f32[4,4,128,24,64]{2,4,3,1,0:T(8,128)}, bf16[4,4,128,24,64]{2,4,3,1,0:T(8,128)(2,1)}, bf16[4,4,128,128]{3,2,1,0:T(8,128)(2,1)S(1)},...) while((s32[]{:T(128)}, ...), condition=%wide.region_3.4_spmd, body=%wide.region_2.3_spmd.sunk | while | flops 225984512 | bytes 5884001 | solution.py:202
  325.7 23.2 %fusion.60 = bf16[16,24,64,128]{3,0,2,1:T(8,128)(2,1)S(1)} fusion(f32[24,64,128]{2,1,0:T(8,128)S(1)} %get-tuple-element.365, f32[16,24]{0,1:T(8,128)S(1)} %copy.335, f32[16,24,64,128]{3,2,1,0:T(8,128)} %fusion.105, f32[16,24]{0,1:T(8,128)S(1)} %copy.333, f32[16,24]{0,1:T(8,128)S(1)} %bitcast.389, pred[16,16]{1,0:T(8,128)(4,1)S(1)} %iota_compare_fusion.2), kind=kOutput, calls=%fused_computation.109 | convolution fusion | flops 613429248 | bytes 19665664 | tf_op jit(solution)/shard_map/jvp(cdh,dhpn->chpn)/dot_general | solution.py:109
  349.0 23.4 %fusion.61 = (f32[16,128,24,64]{1,3,2,0:T(8,128)}, f32[16,128,24,64]{1,3,2,0:T(8,128)}) fusion(f32[4,4,128,24,64]{2,4,3,1,0:T(8,128)} %get-tuple-element.364, f32[16,128,24,64]{1,0,3,2:T(8,128)} %bitcast.356, f32[24]{0:T(128)S(1)} %copy-done.82, f32[16,128,24]{1,2,0:T(8,128)S(1)} %copy.326, bf16[16,128,128,1]{2,1,3,0:T(8,128)(2,1)S(1)} %copy.388, ...), kind=kOutput, calls=%fused_computation.111 | convolution fusion | flops 817889280 | bytes 57344096 | tf_op jit(solution)/shard_map/btn,bhpn->bthp/dot_general | solution.py:217
  372.4 20.0 %copy.339 = f32[16,128,24,64]{1,0,3,2:T(8,128)} copy(f32[16,128,24,64]{1,3,2,0:T(8,128)} %get-tuple-element.647) | data formatting | bytes 25165824 | tf_op jit(solution)/shard_map/add | solution.py:222
  392.4 15.6 %multiply_reduce_fusion.11 = (f32[2048]{0:T(1024)S(1)}, f32[2048,1536]{0,1:T(8,128)}) fusion(bf16[2048,3352]{0,1:T(8,128)(2,1)} %convolution_convert_fusion, f32[192,8,16,128]{3,2,1,0:T(8,128)} %bitcast.364), kind=kLoop, calls=%fused_computation.126 | loop fusion | flops 25163776 | bytes 31465472 | tf_op jit(solution)/shard_map/jvp()/reduce_sum | solution.py:90
  408.6 14.1 %multiply_reduce_fusion.6 = (f32[1536]{0:T(1024)}, f32[2048]{0:T(1024)S(1)}, f32[2048,1536]{0,1:T(8,128)}) fusion(f32[2048,1536]{0,1:T(8,128)} %get-tuple-element.617, f32[2048]{0:T(1024)} %fusion.158, f32[1536]{0:T(1024)S(1)} %copy-done.68, bf16[1536,768]{1,0:T(8,128)(2,1)} %all-gather.11.cloned.1.call-done, bf16[1,2048,768]{2,1,0:T(8,128)(2,1)} %param.24), kind=kOutput, calls=%fused_computation.117 | convolution fusion | flops 4850708992 | bytes 30699520 | tf_op jit(solution)/shard_map/dot_general | solution.py:244
  424.1 21.8 %fusion.52 = (f32[1536]{0:T(1024)}, bf16[2048,1536]{0,1:T(8,128)(2,1)}, bf16[2048,1536]{0,1:T(8,128)(2,1)}) fusion(bf16[2048,1792]{0,1:T(8,128)(2,1)S(1)} %bitcast.367, bf16[2048,3352]{0,1:T(8,128)(2,1)} %convolution_convert_fusion, f32[2048,1536]{0,1:T(8,128)} %get-tuple-element.617, f32[2048]{0:T(1024)S(1)} %multiply_multiply_fusion.2, ...), kind=kLoop, calls=%fused_computation.96 | loop fusion | flops 75495936 | bytes 62943232 | tf_op jit(solution)/shard_map/reduce_sum | solution.py:250
  445.9 11.0 reshape_reshape.15
  456.9 8.9 convert_bitcast_fusion
  471.9 61.0 %while.61 = (s32[]{:T(128)}, f32[4,4,128,24,64]{2,4,3,1,0:T(8,128)}, f32[4,4,128,128]{3,2,1,0:T(8,128)}, f32[4,4,128,128]{3,2,1,0:T(8,128)}, f32[4,4,128,24]{2,3...) while((s32[]{:T(128)}, ...), condition=%wide.region_15.16_spmd, body=%wide.region_10.15_spmd.sunk | while | flops 481234944 | bytes 14175389 | solution.py:276
  508.6 6.9 fusion.217
  523.7 6.9 fusion.217
  532.9 12.5 %copy.427 = f32[192,8,16,128]{3,2,1,0:T(8,128)} copy(f32[192,8,16,128]{3,1,2,0:T(8,128)} %convert_bitcast_fusion) | data formatting | bytes 25165824
  545.5 13.0 %fusion.106 = f32[16,24,64,128]{3,2,1,0:T(8,128)} fusion(bf16[16,128,128,1]{2,1,3,0:T(8,128)(2,1)S(1)} %copy-done.13, f32[16,128,24,64]{1,0,3,2:T(8,128)} %bitcast.361, f32[16,128,24]{1,2,0:T(8,128)S(1)} %copy-done.15), kind=kOutput, calls=%fused_computation.174 | convolution fusion | flops 811597824 | bytes 25886720 | tf_op jit(solution)/shard_map/bthp,btn->bhpn/dot_general | solution.py:256
  558.5 12.2 %multiply_reduce_fusion.7 = f32[16,24]{0,1:T(8,128)S(1)} fusion(f32[16,24,64,128]{3,2,1,0:T(8,128)} %fusion.106, f32[24,64,128]{2,1,0:T(8,128)S(1)} %copy-done.5), kind=kLoop, calls=%fused_computation.118 | loop fusion | flops 6291072 | bytes 13370880 | tf_op jit(solution)/shard_map/transpose(jvp())/reduce_sum | solution.py:110
  570.6 18.3 %fusion.62 = f32[24,1,64,128]{3,1,2,0:T(1,128)S(1)} fusion(f32[16,24,1,1]{0,2,3,1:T(1,128)S(1)} %copy-done.62, f32[16,24,64,128]{3,2,1,0:T(8,128)} %fusion.106), kind=kOutput, calls=%fused_computation.128 | convolution fusion | flops 37748736 | bytes 13370880 | tf_op jit(solution)/shard_map/bh,bhpn->hpn/dot_general | solution.py:260
  589.8 39.8 %fusion.166 = (f32[16,24]{0,1:T(8,128)S(1)}, f32[16,24]{0,1:T(8,128)S(1)}) fusion(f32[16,24]{0,1:T(8,128)S(1)} %copy-done.46, f32[16,24]{0,1:T(8,128)S(1)} %bitcast.390, f32[16,24,64,128]{3,2,1,0:T(8,128)} %fusion.105, f32[24,64,128,16]{2,1,0,3:T(8,128)} %bitcast.359, pred[16,16]{1,0:T(8,128)(4,1)S(1)} %copy-done.66), kind=kOutput, calls=%fused_computation.263 | convolution fusion | flops 604015872 | bytes 25172224 | tf_op jit(solution)/shard_map/transpose(jvp(cdh,dhpn->chpn))/dot_general | solution.py:109
  632.4 13.9 %fusion.116 = f32[16,128,128]{2,1,0:T(8,128)S(1)} fusion(f32[16,128,128]{2,1,0:T(8,128)} %bitcast.385, bf16[16,24,64,128]{3,0,2,1:T(8,128)(2,1)} %copy-done.2, f32[16,128,24,64]{1,0,3,2:T(8,128)} %bitcast.362, f32[16,128,24]{1,2,0:T(8,128)S(1)} %copy-done.15), kind=kOutput, calls=%fused_computation.178 | convolution fusion | flops 811859968 | bytes 21168128 | tf_op jit(solution)/shard_map/bthp,bhpn->btn/dot_general | solution.py:253
  647.6 10.8 fusion.100
  663.8 25.4 %fusion.69 = f32[24,1,16,1]{2,1,3,0:T(1,128)S(1)} fusion(f32[24,64,128,1]{2,3,1,0:T(1,128)S(1)} %bitcast.369, f32[16,24,64,128]{3,2,1,0:T(8,128)} %fusion.105), kind=kOutput, calls=%fused_computation.135 | convolution fusion | flops 37748736 | bytes 13370880 | tf_op jit(solution)/shard_map/transpose(jvp(dh,dhpn->hpn))/dot_general | solution.py:97
  689.4 25.1 %fusion.81 = bf16[16,24,64,128]{3,0,2,1:T(8,128)(2,1)} fusion(f32[24,16]{1,0:T(8,128)S(1)} %copy.348, f32[24,64,128]{2,1,0:T(8,128)S(1)} %get-tuple-element.367, f32[24,64,128,16]{2,1,0,3:T(8,128)} %bitcast.360, f32[16,24]{0,1:T(8,128)S(1)} %copy-done.46, f32[16,24]{0,1:T(8,128)S(1)} %bitcast.391, pred[16,16]{1,0:T(8,128)(4,1)S(1)} %copy-done.66), kind=kOutput, calls=%fused_computation.153 | convolution fusion | flops 613429248 | bytes 19665664 | tf_op jit(solution)/shard_map/transpose(jvp(cdh,dhpn->chpn))/dot_general | solution.py:109
  716.4 30.4 %fusion.59 = (f32[16,128,24,64]{1,3,2,0:T(8,128)}, f32[16,128,24]{1,2,0:T(8,128)S(1)}, f32[16,128,24]{1,2,0:T(8,128)S(1)}) fusion(f32[4,4,128,24,64]{2,4,3,1,0:T(8,128)} %get-tuple-element.366, f32[16,128,24,64]{1,0,3,2:T(8,128)} %bitcast.363, f32[24]{0:T(128)S(1)} %copy-done.83, f32[16,128,24]{1,2,0:T(8,128)S(1)} %copy-done.24, ...), kind=kOutput, calls=%fused_computation.107 | convolution fusion | flops 833519616 | bytes 70516832 | tf_op jit(solution)/shard_map/bhpn,bsn->bshp/dot_general | solution.py:268
  751.4 23.5 %fusion.172 = f32[16,128,24]{2,0,1:T(8,128)S(1)} fusion(f32[16,128,24]{2,0,1:T(8,128)S(1)} %copy.379), kind=kOutput, calls=%fused_computation.268 | output fusion | flops 6242304 | bytes 393216 | tf_op jit(solution)/shard_map/transpose(jvp(jit(cumsum)))/reduce_window_sum | solution.py:62
  776.1 13.6 %fusion.113 = f32[16,128,128]{2,1,0:T(8,128)S(1)} fusion(f32[16,128,128]{2,1,0:T(8,128)S(1)} %bitcast.384, bf16[16,24,64,128]{3,0,2,1:T(8,128)(2,1)} %fusion.81, f32[16,128,24,64]{1,0,3,2:T(8,128)} %bitcast.358, f32[16,128,24]{1,2,0:T(8,128)S(1)} %copy-done.24), kind=kOutput, calls=%fused_computation.177 | convolution fusion | flops 811859968 | bytes 21168128 | tf_op jit(solution)/shard_map/bhpn,bshp->bsn/dot_general | solution.py:271
  790.0 20.2 %copy.353 = f32[16,128,24,64]{1,0,3,2:T(8,128)} copy(f32[16,128,24,64]{1,3,2,0:T(8,128)} %get-tuple-element.633) | data formatting | bytes 25165824 | tf_op jit(solution)/shard_map/add | solution.py:277
  810.3 15.8 %copy.533 = f32[192,8,16,128]{3,1,2,0:T(8,128)} copy(f32[192,8,16,128]{3,2,1,0:T(8,128)} %bitcast.370) | data formatting | bytes 25165824
  826.1 36.8 %multiply_reduce_fusion.5 = (f32[1792]{0:T(1024)}, f32[1792]{0:T(1024)}, f32[1792]{0:T(1024)}, f32[1792]{0:T(1024)}, f32[1792]{0:T(1024)}, /*index=5*/f32[2048,1792]{0,1:T(8,128)}) fusion(f32[2051,1792]{0,1:T(8,128)} %maximum_convert_fusion, f32[2048,1792]{0,1:T(8,128)} %get-tuple-element.619, f32[2048,128]{0,1:T(8,128)S(1)} %copy-done.20, ...), kind=kLoop, calls=%fused_computation.91 | loop fusion | flops 73391360 | bytes 102796288 | tf_op jit(solution)/shard_map/transpose(jvp())/reduce_sum | solution.py:56
  862.9 19.2 %broadcast_multiply_fusion = (f32[2048,1792]{0,1:T(8,128)S(1)}, f32[2048,1792]{0,1:T(8,128)}, f32[2048,1792]{0,1:T(8,128)}, f32[2048,1792]{0,1:T(8,128)}) fusion(f32[2048,1792]{0,1:T(8,128)} %get-tuple-element.613, f32[1792]{0:T(1024)S(1)} %copy-done.55, f32[1792]{0:T(1024)S(1)} %copy-done.53, f32[1792]{0:T(1024)S(1)} %copy-done.59, f32[1792]{0:T(1024)S(1)} %copy-done.57), kind=kLoop, calls=%fused_computation.145 | loop fusion | flops 14680064 | bytes 73428992 | tf_op jit(solution)/shard_map/transpose(jvp())/mul | solution.py:56
  891.4 21.5 %pad_add_fusion = bf16[2051,1792]{0,1:T(8,128)(2,1)S(1)} fusion(f32[2048,1792]{0,1:T(8,128)} %get-tuple-element.626, f32[2048,1792]{0,1:T(8,128)} %get-tuple-element.627, f32[2048,1792]{0,1:T(8,128)} %get-tuple-element.628, f32[2048,1792]{0,1:T(8,128)} %copy-done), kind=kLoop, calls=%fused_computation.83 | loop fusion | flops 14701568 | bytes 66071040 | tf_op jit(solution)/shard_map/transpose(jvp())/add_any | solution.py:56
  914.7 7.2 slice.141
  933.0 20.3 %fusion.85 = f32[768,3352]{1,0:T(8,128)} fusion(bf16[2048,24]{0,1:T(8,128)(2,1)S(1)} %get-tuple-element.630, bf16[2048,1792]{0,1:T(8,128)(2,1)} %scatter-add.6, bf16[2048,1536]{0,1:T(8,128)(2,1)} %get-tuple-element.624, bf16[1,2048,768]{2,1,0:T(8,128)(2,1)S(1)} %copy-done.6, f32[768]{0:T(1024)S(1)} %copy-done.80, f32[2048]{0:T(1024)S(1)} %copy-done.64), kind=kOutput, calls=%fused_computation.157 | convolution fusion | flops 10591961088 | bytes 27184128 | tf_op jit(solution)/shard_map/dot_general | solution.py:297
  954.1 10.9 fusion.104
  973.4 18.9 %fusion.78 = (f32[768]{0:T(1024)S(1)}, f32[2048]{0:T(1024)S(1)}, f32[2048,768]{1,0:T(8,128)}) fusion(bf16[1,2048,768]{2,1,0:T(8,128)(2,1)S(1)} %copy-done.6, f32[2048]{0:T(1024)S(1)} %copy-done.64, f32[768]{0:T(1024)} %copy-done.79, bf16[768,3352]{1,0:T(8,128)(2,1)} %all-gather.9.cloned.1.call-done, bf16[2048,24]{0,1:T(8,128)(2,1)} %copy-done.51, ...), kind=kOutput, calls=%fused_computation.150 | convolution fusion | flops 10596676608 | bytes 28338176 | tf_op jit(solution)/shard_map/dot_general | solution.py:300
  992.2 41.0 %all-reduce.20 = (f32[768]{0:T(1024)S(1)}, f32[1792,4]{0,1:T(4,128)S(1)}, f32[1792]{0:T(1024)S(1)}, f32[24]{0:T(128)}, f32[24]{0:T(128)}, /*index=5*/f32[24]{0:T(128)}, f32[1536]{0:T(1024)S(1)}) all-reduce(f32[768]{0:T(1024)S(1)} %get-tuple-element.533, ...), channel_id=5, replica_groups=mesh['dp'=8,'seq'=4] {'dp','seq'}, use_global_device_ids=true, to_apply=%region_31.32.clone | all-reduce | flops 11336 | bytes 90688
  1041.7 52.2 %reduce-scatter.8.cloned.1.call-done = f32[24,3352]{1,0:T(8,128)} async-done(((f32[768,3352]{1,0:T(8,128)}), f32[24,3352]{1,0:T(8,128)}) %reduce-scatter.8.cloned.1.call-update) | async-done | bytes 321808
  (402 shorter events, 187.5 us)
Async XLA Ops:
  7.2 91.0 %all-gather.9.cloned.1.call-start = ((), (), s32[]{:S(2)}) async-start(), calls=%async_computation.2 | async-start | bytes 5474304 | tf_op jit(solution)/shard_map/all_gather | solution.py:159
  7.9 312.7 %all-gather.13.cloned.1.call-start = ((), (), s32[]{:S(2)}) async-start(), calls=%async_computation.5 | async-start | bytes 1966080 | tf_op jit(solution)/shard_map/all_gather | solution.py:30
  53.4 62.0 %copy-start.79 = (f32[768]{0:T(1024)}, f32[768]{0:T(1024)S(1)}, u32[]{:S(2)}) copy-start(f32[768]{0:T(1024)S(1)} %convert_element_type.171) | copy-start | bytes 9220
  94.3 72.0 %copy-start.52 = (f32[1792]{0:T(1024)}, f32[1792]{0:T(1024)S(1)}, u32[]{:S(2)}) copy-start(f32[1792]{0:T(1024)S(1)} %get-tuple-element.539) | copy-start | bytes 21508
  94.3 72.0 %copy-start.54 = (f32[1792]{0:T(1024)}, f32[1792]{0:T(1024)S(1)}, u32[]{:S(2)}) copy-start(f32[1792]{0:T(1024)S(1)} %get-tuple-element.540) | copy-start | bytes 21508
  94.3 72.0 %copy-start.56 = (f32[1792]{0:T(1024)}, f32[1792]{0:T(1024)S(1)}, u32[]{:S(2)}) copy-start(f32[1792]{0:T(1024)S(1)} %get-tuple-element.541) | copy-start | bytes 21508
  94.3 72.0 %copy-start.58 = (f32[1792]{0:T(1024)}, f32[1792]{0:T(1024)S(1)}, u32[]{:S(2)}) copy-start(f32[1792]{0:T(1024)S(1)} %get-tuple-element.542) | copy-start | bytes 21508
  117.5 48.7 %copy-start.25 = (f32[3,16,8,128]{3,2,1,0:T(8,128)}, f32[3,16,8,128]{3,2,1,0:T(8,128)S(1)}, u32[]{:S(2)}) copy-start(f32[3,16,8,128]{3,2,1,0:T(8,128)S(1)} %get-tuple-element.632) | copy-start | bytes 589828
  117.6 36.2 %collective-permute-start = (bf16[3,1792]{0,1:T(8,128)(2,1)S(1)}, bf16[3,1792]{0,1:T(8,128)(2,1)}, u32[]{:S(2)}, u32[]{:S(2)}) collective-permute-start(bf16[3,1792]{0,1:T(8,128)(2,1)S(1)} %slice.124), channel_id=1, source_target_pairs={{0,1},{1,2},{2,3},{4,5},{5,6},{6,7},{8,9},{9,10},{10,11},{12,13},{... | collective-permute-start | bytes 32264 | tf_op jit(solution)/shard_map/ppermute | solution.py:24
  145.2 128.2 %copy-start.16 = (f32[16,128,24]{1,2,0:T(8,128)}, f32[16,128,24]{1,2,0:T(8,128)S(1)}, u32[]{:S(2)}) copy-start(f32[16,128,24]{1,2,0:T(8,128)S(1)} %copy.327) | copy-start | bytes 589828
  146.1 81.2 %copy-start.23 = (f32[16,128,24]{1,2,0:T(8,128)}, f32[16,128,24]{1,2,0:T(8,128)S(1)}, u32[]{:S(2)}) copy-start(f32[16,128,24]{1,2,0:T(8,128)S(1)} %fusion.148) | copy-start | bytes 589828
  146.2 127.0 %copy-start.43 = (f32[16,24]{1,0:T(8,128)}, f32[16,24]{1,0:T(8,128)S(1)}, u32[]{:S(2)}) copy-start(f32[16,24]{1,0:T(8,128)S(1)} %reduce_window_sum.65) | copy-start | bytes 4612
  146.2 127.5 %copy-start.49 = (f32[16,24]{1,0:T(8,128)}, f32[16,24]{1,0:T(8,128)S(1)}, u32[]{:S(2)}) copy-start(f32[16,24]{1,0:T(8,128)S(1)} %get-tuple-element.645) | copy-start | bytes 4612
  260.2 148.4 %all-gather.11.cloned.1.call-start = ((), (), s32[]{:S(2)}) async-start(), calls=%async_computation.3 | async-start | bytes 2433024 | tf_op jit(solution)/shard_map/all_gather | solution.py:163
  261.0 397.6 %all-gather.15.cloned.1.call-start = ((), (), s32[]{:S(2)}) async-start(), calls=%async_computation.6 | async-start | bytes 1966080 | tf_op jit(solution)/shard_map/all_gather | solution.py:30
  261.0 64.7 %copy-start.65 = (pred[16,16]{1,0:T(8,128)(4,1)}, pred[16,16]{1,0:T(8,128)(4,1)S(1)}, u32[]{:S(2)}) copy-start(pred[16,16]{1,0:T(8,128)(4,1)S(1)} %iota_compare_fusion.2) | copy-start | bytes 772
  264.1 61.6 %copy-start.45 = (f32[16,24]{0,1:T(8,128)}, f32[16,24]{0,1:T(8,128)S(1)}, u32[]{:S(2)}) copy-start(f32[16,24]{0,1:T(8,128)S(1)} %copy.333) | copy-start | bytes 4612
  266.6 82.4 %copy-start.14 = (f32[16,128,24]{1,2,0:T(8,128)}, f32[16,128,24]{1,2,0:T(8,128)S(1)}, u32[]{:S(2)}) copy-start(f32[16,128,24]{1,2,0:T(8,128)S(1)} %copy.326) | copy-start | bytes 589828
  273.7 52.0 %copy-start.47 = (f32[16,1,24]{0,2,1:T(8,128)}, f32[16,1,24]{0,2,1:T(8,128)S(1)}, u32[]{:S(2)}) copy-start(f32[16,1,24]{0,2,1:T(8,128)S(1)} %copy.403) | copy-start | bytes 4612
  320.0 29.0 %copy-start.7 = (bf16[4,4,128,128]{3,2,1,0:T(8,128)(2,1)}, bf16[4,4,128,128]{3,2,1,0:T(8,128)(2,1)S(1)}, u32[]{:S(2)}) copy-start(bf16[4,4,128,128]{3,2,1,0:T(8,128)(2,1)S(1)} %get-tuple-element.962) | copy-start | bytes 1572868
  320.0 29.0 %copy-start.9 = (bf16[4,4,128,128]{3,2,1,0:T(8,128)(2,1)}, bf16[4,4,128,128]{3,2,1,0:T(8,128)(2,1)S(1)}, u32[]{:S(2)}) copy-start(bf16[4,4,128,128]{3,2,1,0:T(8,128)(2,1)S(1)} %get-tuple-element.963) | copy-start | bytes 1572868
  320.6 28.4 %copy-start.12 = (bf16[16,128,128,1]{2,1,3,0:T(8,128)(2,1)}, bf16[16,128,128,1]{2,1,3,0:T(8,128)(2,1)S(1)}, u32[]{:S(2)}) copy-start(bf16[16,128,128,1]{2,1,3,0:T(8,128)(2,1)S(1)} %copy.388) | copy-start | bytes 1572868
  320.6 28.4 %copy-start.82 = (f32[24]{0:T(128)S(1)}, f32[24]{0:T(128)}, u32[]{:S(2)}) copy-start(f32[24]{0:T(128)} %param.31) | copy-start | bytes 292
  325.7 46.7 %copy-start.4 = (f32[24,64,128]{2,1,0:T(8,128)}, f32[24,64,128]{2,1,0:T(8,128)S(1)}, u32[]{:S(2)}) copy-start(f32[24,64,128]{2,1,0:T(8,128)S(1)} %get-tuple-element.365) | copy-start | bytes 2359300
  325.7 46.7 %copy-start.93 = (bf16[4,24]{1,0:T(4,128)(2,1)}, bf16[4,24]{1,0:T(4,128)(2,1)S(1)}, u32[]{:S(2)}) copy-start(bf16[4,24]{1,0:T(4,128)(2,1)S(1)} %get-tuple-element.989) | copy-start | bytes 580
  392.4 30.3 %slice-start = ((s8[7340032]{0:T(1024)(128)(4,1)}), s8[3145728]{0:T(1024)(128)(4,1)S(1)}, s32[]{:S(2)}) async-start(s8[7340032]{0:T(1024)(128)(4,1)} %bitcast.366), calls=%async_computation.8 | async-start | bytes 6291456
  532.9 98.7 %copy-start.32 = (f32[4,4,128,24]{2,3,1,0:T(8,128)}, f32[4,4,128,24]{2,3,1,0:T(8,128)S(1)}, u32[]{:S(2)}) copy-start(f32[4,4,128,24]{2,3,1,0:T(8,128)S(1)} %get-tuple-element.370) | copy-start | bytes 589828
  558.5 31.4 %copy-start.46 = (f32[16,24]{0,1:T(8,128)S(1)}, f32[16,24]{0,1:T(8,128)}, u32[]{:S(2)}) copy-start(f32[16,24]{0,1:T(8,128)} %copy-done.45) | copy-start | bytes 4612
  558.5 31.4 %copy-start.48 = (f32[16,1,24]{0,2,1:T(8,128)S(1)}, f32[16,1,24]{0,2,1:T(8,128)}, u32[]{:S(2)}) copy-start(f32[16,1,24]{0,2,1:T(8,128)} %copy-done.47) | copy-start | bytes 4612
  558.5 31.4 %copy-start.66 = (pred[16,16]{1,0:T(8,128)(4,1)S(1)}, pred[16,16]{1,0:T(8,128)(4,1)}, u32[]{:S(2)}) copy-start(pred[16,16]{1,0:T(8,128)(4,1)} %copy-done.65) | copy-start | bytes 772
  589.8 451.9 %reduce-scatter.6.cloned.1.call-start = ((), (), s32[]{:S(2)}) async-start(), calls=%async_computation.4 | async-start | bytes 4866048 | tf_op jit(solution)/shard_map/reduce_scatter | solution.py:311
  658.4 30.8 %copy-start.44 = (f32[16,24]{1,0:T(8,128)S(1)}, f32[16,24]{1,0:T(8,128)}, u32[]{:S(2)}) copy-start(f32[16,24]{1,0:T(8,128)} %copy-done.43) | copy-start | bytes 4612
  658.4 30.8 %copy-start.86 = (f32[24]{0:T(128)S(1)}, f32[24]{0:T(128)}, u32[]{:S(2)}) copy-start(f32[24]{0:T(128)} %copy-done.85) | copy-start | bytes 292
  658.5 435.5 %reduce-scatter.8.cloned.1.call-start = ((), (), s32[]{:S(2)}) async-start(), calls=%async_computation.7 | async-start | bytes 10948608
  716.3 30.5 %copy-start.17 = (f32[16,128,24]{1,2,0:T(8,128)S(1)}, f32[16,128,24]{1,2,0:T(8,128)}, u32[]{:S(2)}) copy-start(f32[16,128,24]{1,2,0:T(8,128)} %copy-done.16) | copy-start | bytes 589828
  716.3 30.5 %copy-start.26 = (f32[3,16,8,128]{3,2,1,0:T(8,128)S(1)}, f32[3,16,8,128]{3,2,1,0:T(8,128)}, u32[]{:S(2)}) copy-start(f32[3,16,8,128]{3,2,1,0:T(8,128)} %copy-done.25) | copy-start | bytes 589828
  716.3 30.5 %copy-start.41 = (f32[16,24]{1,0:T(8,128)S(1)}, f32[16,24]{1,0:T(8,128)}, u32[]{:S(2)}) copy-start(f32[16,24]{1,0:T(8,128)} %copy-done.40) | copy-start | bytes 4612
  716.3 30.5 %copy-start.78 = (f32[24]{0:T(128)S(1)}, f32[24]{0:T(128)}, u32[]{:S(2)}) copy-start(f32[24]{0:T(128)} %param.29) | copy-start | bytes 292
  716.4 31.0 %copy-start.34 = (f32[16,1,24]{1,2,0:T(8,128)S(1)}, f32[16,1,24]{1,2,0:T(8,128)}, u32[]{:S(2)}) copy-start(f32[16,1,24]{1,2,0:T(8,128)} %copy-done.33) | copy-start | bytes 4612
  716.4 31.0 %copy-start.38 = (f32[16,1,24]{1,2,0:T(8,128)S(1)}, f32[16,1,24]{1,2,0:T(8,128)}, u32[]{:S(2)}) copy-start(f32[16,1,24]{1,2,0:T(8,128)} %copy.371) | copy-start | bytes 4612
  716.4 59.7 %copy-start.35 = (f32[4,4,128,128]{3,2,1,0:T(8,128)S(1)}, f32[4,4,128,128]{3,2,1,0:T(8,128)}, u32[]{:S(2)}) copy-start(f32[4,4,128,128]{3,2,1,0:T(8,128)} %get-tuple-element.368) | copy-start | bytes 3145732
  826.1 36.8 %copy-start.53 = (f32[1792]{0:T(1024)S(1)}, f32[1792]{0:T(1024)}, u32[]{:S(2)}) copy-start(f32[1792]{0:T(1024)} %copy-done.52) | copy-start | bytes 21508
  826.1 36.8 %copy-start.55 = (f32[1792]{0:T(1024)S(1)}, f32[1792]{0:T(1024)}, u32[]{:S(2)}) copy-start(f32[1792]{0:T(1024)} %copy-done.54) | copy-start | bytes 21508
  826.1 36.8 %copy-start.57 = (f32[1792]{0:T(1024)S(1)}, f32[1792]{0:T(1024)}, u32[]{:S(2)}) copy-start(f32[1792]{0:T(1024)} %copy-done.56) | copy-start | bytes 21508
  826.1 36.8 %copy-start.59 = (f32[1792]{0:T(1024)S(1)}, f32[1792]{0:T(1024)}, u32[]{:S(2)}) copy-start(f32[1792]{0:T(1024)} %copy-done.58) | copy-start | bytes 21508
  890.0 32.0 %collective-permute-start.1 = (f32[3,1792]{1,0:T(4,128)S(1)}, f32[3,1792]{1,0:T(4,128)S(1)}, u32[]{:S(2)}, u32[]{:S(2)}) collective-permute-start(f32[3,1792]{1,0:T(4,128)S(1)} %copy.358), channel_id=1, source_target_pairs={{1,0},{2,1},{3,2},{5,4},{6,5},{7,6},{9,8},{10,9},{11,10},{13,12},{... | collective-permute-start | bytes 64520 | tf_op jit(solution)/shard_map/ppermute | solution.py:24
  973.3 62.3 %copy-start.61 = (f32[2048]{0:T(1024)S(1)}, f32[2048]{0:T(1024)}, u32[]{:S(2)}) copy-start(f32[2048]{0:T(1024)} %copy-done.60) | copy-start | bytes 24580
  973.3 62.3 %copy-start.81 = (f32[768]{0:T(1024)S(1)}, f32[768]{0:T(1024)}, u32[]{:S(2)}) copy-start(f32[768]{0:T(1024)} %copy-done.79) | copy-start | bytes 9220
  (58 other events, 976.9 us)
Sparse Core Ops, SparseCore 0:
  10.8 68.4 all-gather.8
  260.3 15.6 all-gather.12
  279.0 57.2 all-gather.10
  589.9 16.2 all-gather.14
  658.6 103.2 reduce-scatter.5
  953.4 140.4 reduce-scatter.7
where the time goes:
time: 1110 us; the launch traced here: 1100 us
  matrix products  422 us (38%)
  other arithmetic  280 us (25%)
  local copies, waits for them, and re-layouts  192 us (17%)
  blocking collectives  131 us (12%)
  waiting for transfers between devices  53.7 us (5%)
  between operations  16.4 us (1%)
    unnamed x3, blocking collectives  90 us
    dot_general x3, matrix products, state_chain(): within = jnp.einsum('cdh,dhpn->chpn', factor, states, precision=HIGHEST)  88.1 us
    unnamed x215, local copies, waits for them, and re-layouts  56.7 us
    unnamed x7, waiting for transfers between devices  53.7 us
    another operation x2, other arithmetic, make_steps(): cumulative = jnp.cumsum(step_vals * -jnp.exp(decay_log), axis=1)  46.8 us
    dot_general x2, matrix products, outgoing(): return jnp.einsum('dh,dhpn->hpn', tail_decay, states, precision=HIGHEST)  44.1 us
    all_gather x1, blocking collectives, on_device(): lax.all_gather(conv_weight, ('dp', 'seq'), axis=0, tiled=True)  40.7 us
    reduce_sum x1, other arithmetic, conv_apply(): extended[offset:offset + seq_len] * weight[:, offset]  36.8 us
  transfers between devices with their start and end apart: 8, of which 1 were waited for; matrix products, arithmetic and copies ran while one was open for 53% of the time, Pallas kernels for 0%

commit v1 on v0

v1 whole, which is shorter than its diff:
```python
import functools

import jax
import jax.numpy as jnp
import numpy as np
from jax import lax
from jax.experimental import pallas as pl
from jax.experimental.pallas import tpu as pltpu
from jax.sharding import PartitionSpec as P

D = 768
HEADS = 24
HEADDIM = 64
NSTATE = 128
CONV = 4
BLOCK = 128
DI = 1536
CH = 1792
PAIRS = HEADS // 2
EPS = 1e-05
LOG2E = 1.4426950408889634
F32 = jnp.float32
BF16 = jnp.bfloat16
NT = (((1,), (1,)), ((), ()))
VMEM_LIMIT = 60 * 1024 * 1024


def dot(a, b):
    return jnp.dot(a, b, preferred_element_type=F32)


def dot_nt(a, b):
    return lax.dot_general(a, b, NT, preferred_element_type=F32)


def dot_exact(a, b):
    return jnp.dot(a, b, preferred_element_type=F32, precision=lax.Precision.HIGHEST)


def sigmoid(v):
    return 0.5 * jnp.tanh(0.5 * v) + 0.5


def iota(shape, dim):
    return lax.broadcasted_iota(jnp.int32, shape, dim)


def lane_lo():
    return iota((BLOCK, BLOCK), 1) < HEADDIM


def expand_pair(x, j, lo):
    rows = x.shape[0]
    a = jnp.broadcast_to(x[:, 2 * j : 2 * j + 1], (rows, BLOCK))
    b = jnp.broadcast_to(x[:, 2 * j + 1 : 2 * j + 2], (rows, BLOCK))
    return jnp.where(lo, a, b), a, b


def block_diag(v):
    lo = iota(v.shape, 1) < HEADDIM
    zero = jnp.zeros_like(v)
    return jnp.concatenate([jnp.where(lo, v, zero), jnp.where(lo, zero, v)], axis=0)


def pair(j):
    return slice(j * BLOCK, (j + 1) * BLOCK)


def rms_rows(tok, gain):
    x = tok.astype(F32)
    inv = lax.rsqrt(jnp.mean(x * x, axis=-1, keepdims=True) + EPS)
    return (x * inv * gain).astype(BF16)


def first_kernel(
    T, tok_ref, halo_ref, wc_ref, gain_ref, conv_ref, head_ref,
    normed_ref, convin_ref, act_ref, dt_ref, cum_ref, sig_ref, bst_ref, leave_ref, tot_ref,
    ext, state, weighted,
):
    i = pl.program_id(0)

    @pl.when(i == 0)
    def _():
        hn = rms_rows(halo_ref[...], gain_ref[...])
        hp = dot(hn, wc_ref[:, :CH]).astype(BF16).astype(F32)
        ext[0:8] = hp[8:16]
        state[...] = jnp.zeros_like(state)
        tot_ref[...] = jnp.zeros_like(tot_ref)

    @pl.when(i > 0)
    def _():
        ext[0:8] = ext[T : T + 8]

    normed = rms_rows(tok_ref[...], gain_ref[...])
    normed_ref[...] = normed
    for c in range(CH // 256):
        cs = slice(c * 256, (c + 1) * 256)
        p = dot(normed, wc_ref[:, cs]).astype(BF16)
        convin_ref[:, cs] = p
        ext[8 : 8 + T, cs] = p.astype(F32)
        total = conv_ref[4:5, cs]
        for k in range(CONV):
            total = total + ext[5 + k : 5 + k + T, cs] * conv_ref[k : k + 1, cs]
        act_ref[:, cs] = (total * sigmoid(total)).astype(BF16)
    raw = dot(normed, wc_ref[:, CH:]).astype(BF16).astype(F32) + head_ref[0:1]
    dt_all = jnp.maximum(raw, 0.0) + jnp.log1p(jnp.exp(-jnp.abs(raw)))
    dt_ref[...] = dt_all
    sig_ref[...] = sigmoid_exact(raw)
    tril = (iota((BLOCK, BLOCK), 0) >= iota((BLOCK, BLOCK), 1)).astype(F32)
    lo = lane_lo()
    for blk in range(T // BLOCK):
        rows = slice(blk * BLOCK, (blk + 1) * BLOCK)
        dt = dt_all[rows]
        cum = dot_exact(tril, dt * head_ref[1:2]) * LOG2E
        cum_ref[rows] = cum
        end = cum[BLOCK - 1 : BLOCK]
        tot_ref[...] += jnp.broadcast_to(end, tot_ref.shape)
        wfac = jnp.exp2(end - cum) * dt
        decay = jnp.broadcast_to(jnp.exp2(end), (8, BLOCK))
        write_t = act_ref[rows, DI : DI + NSTATE].T
        for j in range(PAIRS):
            w, _, _ = expand_pair(wfac, j, lo)
            weighted[:, pair(j)] = (act_ref[rows, pair(j)].astype(F32) * w).astype(BF16)
        for q in range(PAIRS // 2):
            cs = slice(q * 256, (q + 1) * 256)
            new = dot(write_t, weighted[:, cs])
            bst_ref[blk, :, cs] = new.astype(BF16)
            d0, _, _ = expand_pair(decay, 2 * q, lo[:8])
            d1, _, _ = expand_pair(decay, 2 * q + 1, lo[:8])
            dd = jnp.concatenate([d0, d1], axis=1)[0:1]
            state[:, cs] = state[:, cs] * dd + new

    @pl.when(i == pl.num_programs(0) - 1)
    def _():
        leave_ref[...] = state[...]


def sigmoid_exact(v):
    return 1.0 / (1.0 + jnp.exp(-v))


def second_kernel(
    T, normed_ref, act_ref, dt_ref, cum_ref, bst_ref, inc_ref, tok_ref, cot_ref, wg_ref, wo_ref, row_ref, et_ref,
    mixed_ref, nout_ref, ggrad_ref, mlow_ref, dcum_ref, ent_ref, egrad_ref, rg_ref, leave_ref, back_ref, cols_ref,
    gate_s, ng, ms, growth, rlow, prod, plow, state, exg, lows,
):
    i = pl.program_id(0)

    @pl.when(i == 0)
    def _():
        state[...] = inc_ref[...]
        exg[...] = jnp.ones_like(exg)
        back_ref[...] = jnp.zeros_like(back_ref)
        cols_ref[...] = jnp.zeros_like(cols_ref)

    lo = lane_lo()
    for c in range(DI // 256):
        cs = slice(c * 256, (c + 1) * 256)
        gate_s[:, cs] = dot(normed_ref[...], wg_ref[:, cs]).astype(BF16)
        ng[:, cs] = dot_nt(cot_ref[...], wo_ref[cs, :])
    lower = iota((BLOCK, BLOCK), 0) >= iota((BLOCK, BLOCK), 1)
    nblk = T // BLOCK
    for blk in range(nblk):
        rows = slice(blk * BLOCK, (blk + 1) * BLOCK)
        cum = cum_ref[rows]
        cum_t = cum.T
        dt = dt_ref[rows]
        write = act_ref[rows, DI : DI + NSTATE]
        read = act_ref[rows, DI + NSTATE :]
        inner = jnp.where(lower, dot_nt(read, write), 0.0)
        lows[blk] = state[...].astype(BF16)
        ent_ref[blk] = lows[blk]
        for j in range(PAIRS):
            cols, a, b = expand_pair(cum, j, lo)
            ga = jnp.exp2(jnp.minimum(a - cum_t[2 * j : 2 * j + 1], 0.0)) * inner
            gb = jnp.exp2(jnp.minimum(b - cum_t[2 * j + 1 : 2 * j + 2], 0.0)) * inner
            scores = jnp.concatenate([ga.astype(BF16), gb.astype(BF16)], axis=1)
            vals = act_ref[rows, pair(j)].astype(F32)
            dtp, _, _ = expand_pair(dt, j, lo)
            vdt = (vals * dtp).astype(BF16)
            grow = jnp.exp2(cols)
            growth[rows, pair(j)] = grow
            diag = dot(scores, block_diag(vdt))
            out = dot(read, lows[blk, :, pair(j)])
            ms[rows, pair(j)] = diag + grow * out + row_ref[1:2, pair(j)] * vals
            dec = grow[BLOCK - 1 : BLOCK]
            state[:, pair(j)] = state[:, pair(j)] * dec + bst_ref[blk, :, pair(j)].astype(F32)

    sq = jnp.zeros((T, BLOCK), F32)
    ug = jnp.zeros((T, BLOCK), F32)
    for j in range(PAIRS):
        g = gate_s[:, pair(j)].astype(F32)
        gated = ms[:, pair(j)] * (g * sigmoid(g))
        sq = sq + gated * gated
        ug = ug + gated * (ng[:, pair(j)] * row_ref[0:1, pair(j)])
    inv = lax.rsqrt(jnp.sum(sq, axis=-1, keepdims=True) * (1.0 / DI) + EPS)
    coef = jnp.sum(ug, axis=-1, keepdims=True) * (1.0 / DI) * (inv * inv * inv)
    for j in range(PAIRS):
        g = gate_s[:, pair(j)].astype(F32)
        sg = sigmoid(g)
        silu = g * sg
        m = ms[:, pair(j)]
        gated = m * silu
        n = ng[:, pair(j)]
        gain = row_ref[0:1, pair(j)]
        gi = gated * inv
        nout_ref[:, pair(j)] = (gi * gain).astype(BF16)
        dg = inv * (n * gain) - gated * coef
        low = (dg * silu).astype(BF16)
        mlow_ref[:, pair(j)] = low
        ggrad_ref[:, pair(j)] = (dg * m * (sg + silu * (1.0 - sg))).astype(BF16)
        vals = act_ref[:, pair(j)].astype(F32)
        lowf = low.astype(F32)
        mv = lowf * vals
        pr = lowf * m - row_ref[1:2, pair(j)] * mv
        hi = pr.astype(BF16)
        prod[:, pair(j)] = hi
        plow[:, pair(j)] = (pr - hi.astype(F32)).astype(BF16)
        rlow[:, pair(j)] = (lowf * growth[:, pair(j)]).astype(BF16)
        cols_ref[0:8, pair(j)] += jnp.sum((n * gi).reshape(T // 8, 8, BLOCK), axis=0)
        cols_ref[8:16, pair(j)] += jnp.sum(mv.reshape(T // 8, 8, BLOCK), axis=0)
    dcum_ref[...] = dot(prod[...], et_ref[...]) + dot(plow[...], et_ref[...])
    mixed_ref[...] = (tok_ref[...].astype(F32) + dot(nout_ref[...], wo_ref[...])).astype(BF16)
    for blk in range(nblk):
        rows = slice(blk * BLOCK, (blk + 1) * BLOCK)
        read_t = act_ref[rows, DI + NSTATE :].T
        for q in range(PAIRS // 2):
            cs = slice(q * 256, (q + 1) * 256)
            eg = dot(read_t, rlow[rows, cs])
            egrad_ref[blk, :, cs] = eg.astype(BF16)
            back_ref[:, cs] += eg * exg[0:1, cs]
        exg[...] = exg[...] * growth[blk * BLOCK + BLOCK - 1 : blk * BLOCK + BLOCK, :]
        rg_ref[rows] = dot_nt(rlow[rows, :], lows[blk])

    @pl.when(i == pl.num_programs(0) - 1)
    def _():
        leave_ref[...] = state[...].astype(BF16)


def third_kernel(
    T, act_ref, convin_ref, prev_ref, halo_ref, dt_ref, cum_ref, sig_ref, dcum_ref, mlow_ref, ent_ref, leave_ref,
    egrad_ref, rg_ref, inc_ref, row_ref, conv_ref, head_ref, et_ref,
    pg_ref, raw_ref, cgrad_ref, hgrad_ref, gfirst_ref, glast_ref,
    carry, dact, vprod, prod, plow, weighted, lows, dec, nxt, gext, cext,
):
    i = pl.program_id(0)
    steps = pl.num_programs(0)

    @pl.when(i == 0)
    def _():
        carry[...] = inc_ref[...]
        nxt[...] = leave_ref[...]
        cgrad_ref[...] = jnp.zeros_like(cgrad_ref)
        hgrad_ref[...] = jnp.zeros_like(hgrad_ref)
        gext[T : T + 8] = jnp.zeros((8, CH), F32)

    @pl.when(i > 0)
    def _():
        gext[T : T + 8] = gext[0:8]

    @pl.when(i == steps - 1)
    def _():
        cext[0:16] = halo_ref[...].astype(F32)

    @pl.when(i < steps - 1)
    def _():
        cext[0:16] = prev_ref[...].astype(F32)

    lo = lane_lo()
    upper = iota((BLOCK, BLOCK), 0) <= iota((BLOCK, BLOCK), 1)
    triu = upper.astype(F32)
    last = iota((BLOCK, BLOCK), 0) == BLOCK - 1
    for blk in reversed(range(T // BLOCK)):
        rows = slice(blk * BLOCK, (blk + 1) * BLOCK)
        cum = cum_ref[rows]
        cum_t = cum.T
        dt = dt_ref[rows]
        end = cum[BLOCK - 1 : BLOCK]
        rest = end - cum
        write = act_ref[rows, DI : DI + NSTATE]
        read = act_ref[rows, DI + NSTATE :]
        inner = jnp.where(upper, dot_nt(write, read), 0.0)
        lows[...] = carry[...].astype(BF16)
        acc = jnp.zeros((BLOCK, BLOCK), F32)
        for j in range(PAIRS):
            cols, a, b = expand_pair(cum, j, lo)
            wexp, _, _ = expand_pair(rest, j, lo)
            wexp = jnp.exp2(wexp)
            da = jnp.exp2(jnp.minimum(cum_t[2 * j : 2 * j + 1] - a, 0.0))
            db = jnp.exp2(jnp.minimum(cum_t[2 * j + 1 : 2 * j + 2] - b, 0.0))
            scores = jnp.concatenate([(da * inner).astype(BF16), (db * inner).astype(BF16)], axis=1)
            m = mlow_ref[rows, pair(j)]
            diag = block_diag(m)
            z = dot(scores, diag)
            vals = act_ref[rows, pair(j)].astype(F32)
            dtp, _, _ = expand_pair(dt, j, lo)
            vdt = vals * dtp
            vdtb = vdt.astype(BF16)
            wtb = (vdt * wexp).astype(BF16)
            g = dot_nt(vdtb, diag)
            acc = acc + g[:, :BLOCK] * da + g[:, BLOCK:] * db
            wg = dot(write, lows[:, pair(j)])
            pr = vdtb.astype(F32) * z + wtb.astype(F32) * wg
            z = z + wg * wexp
            dact[rows, pair(j)] = row_ref[1:2, pair(j)] * m.astype(F32) + dtp * z
            vprod[:, pair(j)] = (vals * z).astype(BF16)
            hi = pr.astype(BF16)
            prod[:, pair(j)] = hi
            plow[:, pair(j)] = (pr - hi.astype(F32)).astype(BF16)
            weighted[:, pair(j)] = wtb
            dec[0:1, pair(j)] = jnp.exp2(cols[BLOCK - 1 : BLOCK])
        low = jnp.where(upper, acc, 0.0).astype(BF16)
        dact[rows, DI : DI + NSTATE] = dot_nt(weighted[...], lows[...]) + dot(low, read)
        dact[rows, DI + NSTATE :] = rg_ref[rows] + dot(low.T, write)
        c = dot(vprod[...], et_ref[...])
        used = dot(prod[...], et_ref[...]) + dot(plow[...], et_ref[...])
        ends = jnp.sum((lows[...].astype(F32) * nxt[...].astype(F32)).reshape(16, 8, DI), axis=0)
        ends_hi = ends.astype(BF16)
        ends_lo = (ends - ends_hi.astype(F32)).astype(BF16)
        de = jnp.sum(dot(ends_hi, et_ref[...]) + dot(ends_lo, et_ref[...]), axis=0, keepdims=True)
        dc = dcum_ref[rows] - used + jnp.where(last, de, 0.0)
        da_log = dot_exact(triu, dc)
        draw = (c + da_log * head_ref[1:2]) * sig_ref[rows]
        raw_ref[rows] = draw.astype(BF16)
        hgrad_ref[0:8] += jnp.sum(draw.reshape(16, 8, BLOCK), axis=0)
        hgrad_ref[8:16] += jnp.sum((da_log * dt).reshape(16, 8, BLOCK), axis=0) * head_ref[1:2]
        nxt[...] = ent_ref[blk]
        for q in range(PAIRS // 2):
            cs = slice(q * 256, (q + 1) * 256)
            carry[:, cs] = carry[:, cs] * dec[0:1, cs] + egrad_ref[blk, :, cs].astype(F32)

    for c in range(CH // 128):
        cs = slice(c * 128, (c + 1) * 128)
        cext[16 : 16 + T, cs] = convin_ref[:, cs].astype(F32)
        taps = [cext[13 + k : 13 + k + T, cs] for k in range(CONV)]
        pre = conv_ref[4:5, cs]
        for k in range(CONV):
            pre = pre + taps[k] * conv_ref[k : k + 1, cs]
        sg = sigmoid(pre)
        g = dact[:, cs] * (sg * (1.0 + pre * (1.0 - sg)))
        gext[0:T, cs] = g
        for k in range(CONV):
            cgrad_ref[8 * k : 8 * k + 8, cs] += jnp.sum((g * taps[k]).reshape(T // 8, 8, BLOCK), axis=0)
        cgrad_ref[32:40, cs] += jnp.sum(g.reshape(T // 8, 8, BLOCK), axis=0)
        back = g * conv_ref[3:4, cs]
        for k in range(CONV - 1):
            back = back + gext[3 - k : 3 - k + T, cs] * conv_ref[k : k + 1, cs]
        pg_ref[:, cs] = back.astype(BF16)

        @pl.when(i == 0)
        def _():
            glast_ref[:, cs] = back[T - 8 :]

    @pl.when(i == steps - 1)
    def _():
        gfirst_ref[...] = gext[0:8]


def full(shape):
    return pl.BlockSpec(shape, lambda i: (0,) * len(shape))


def params():
    return pltpu.CompilerParams(dimension_semantics=("arbitrary",), vmem_limit_bytes=VMEM_LIMIT)


def head_columns():
    et = np.zeros((DI, BLOCK), np.float32)
    et[np.arange(DI), np.arange(DI) // HEADDIM] = 1.0
    return et


def sds(shape, dtype):
    return jax.ShapeDtypeStruct(shape, dtype)


def first_pass(tok, halo, wc, gain, conv, head, T=256):
    L = tok.shape[0]
    nb, per = L // BLOCK, T // BLOCK
    row = lambda w: pl.BlockSpec((T, w), lambda i: (i, 0))
    return pl.pallas_call(
        functools.partial(first_kernel, T),
        grid=(L // T,),
        in_specs=[row(D), full((16, D)), full((D, CH + BLOCK)), full((1, D)), full((8, CH)), full((8, BLOCK))],
        out_specs=[
            row(D), row(CH), row(CH), row(BLOCK), row(BLOCK), row(BLOCK),
            pl.BlockSpec((per, NSTATE, DI), lambda i: (i, 0, 0)), full((NSTATE, DI)), full((8, BLOCK)),
        ],
        out_shape=[
            sds((L, D), BF16), sds((L, CH), BF16), sds((L, CH), BF16), sds((L, BLOCK), F32), sds((L, BLOCK), F32),
            sds((L, BLOCK), F32), sds((nb, NSTATE, DI), BF16), sds((NSTATE, DI), F32), sds((8, BLOCK), F32),
        ],
        scratch_shapes=[
            pltpu.VMEM((T + 8, CH), F32), pltpu.VMEM((NSTATE, DI), F32), pltpu.VMEM((BLOCK, DI), BF16),
        ],
        compiler_params=params(),
        name="first_pass",
    )(tok, halo, wc, gain, conv, head)


def second_pass(normed, act, dt, cum, bst, inc, tok, cot, wg, wo, rows, et, T=256):
    L = tok.shape[0]
    nb, per = L // BLOCK, T // BLOCK
    row = lambda w: pl.BlockSpec((T, w), lambda i: (i, 0))
    blk = pl.BlockSpec((per, NSTATE, DI), lambda i: (i, 0, 0))
    return pl.pallas_call(
        functools.partial(second_kernel, T),
        grid=(L // T,),
        in_specs=[
            row(D), row(CH), row(BLOCK), row(BLOCK), blk, full((NSTATE, DI)), row(D), row(D), full((D, DI)),
            full((DI, D)), full((8, DI)), full((DI, BLOCK)),
        ],
        out_specs=[
            row(D), row(DI), row(DI), row(DI), row(BLOCK), blk, blk, row(BLOCK), full((NSTATE, DI)),
            full((NSTATE, DI)), full((16, DI)),
        ],
        out_shape=[
            sds((L, D), BF16), sds((L, DI), BF16), sds((L, DI), BF16), sds((L, DI), BF16), sds((L, BLOCK), F32),
            sds((nb, NSTATE, DI), BF16), sds((nb, NSTATE, DI), BF16), sds((L, BLOCK), F32), sds((NSTATE, DI), BF16),
            sds((NSTATE, DI), F32), sds((16, DI), F32),
        ],
        scratch_shapes=[
            pltpu.VMEM((T, DI), BF16), pltpu.VMEM((T, DI), F32), pltpu.VMEM((T, DI), F32), pltpu.VMEM((T, DI), F32),
            pltpu.VMEM((T, DI), BF16), pltpu.VMEM((T, DI), BF16), pltpu.VMEM((T, DI), BF16), pltpu.VMEM((NSTATE, DI), F32),
            pltpu.VMEM((8, DI), F32), pltpu.VMEM((per, NSTATE, DI), BF16),
        ],
        compiler_params=params(),
        name="second_pass",
    )(normed, act, dt, cum, bst, inc, tok, cot, wg, wo, rows, et)


def third_pass(act, convin, halo, dt, cum, sig, dcum, mlow, ent, leave, egrad, rg, inc, rows, conv, head, et, T=256):
    L = act.shape[0]
    n, per = L // T, T // BLOCK
    row = lambda w: pl.BlockSpec((T, w), lambda i: (n - 1 - i, 0))
    blk = pl.BlockSpec((per, NSTATE, DI), lambda i: (n - 1 - i, 0, 0))
    prev = pl.BlockSpec((16, CH), lambda i: (jnp.maximum((n - 1 - i) * (T // 16) - 1, 0), 0))
    return pl.pallas_call(
        functools.partial(third_kernel, T),
        grid=(n,),
        in_specs=[
            row(CH), row(CH), prev, full((16, CH)), row(BLOCK), row(BLOCK), row(BLOCK), row(BLOCK), row(DI), blk,
            full((NSTATE, DI)), blk, row(BLOCK), full((NSTATE, DI)), full((8, DI)), full((8, CH)), full((8, BLOCK)),
            full((DI, BLOCK)),
        ],
        out_specs=[row(CH), row(BLOCK), full((40, CH)), full((16, BLOCK)), full((8, CH)), full((8, CH))],
        out_shape=[
            sds((L, CH), BF16), sds((L, BLOCK), BF16), sds((40, CH), F32), sds((16, BLOCK), F32), sds((8, CH), F32),
            sds((8, CH), F32),
        ],
        scratch_shapes=[
            pltpu.VMEM((NSTATE, DI), F32), pltpu.VMEM((T, CH), F32), pltpu.VMEM((BLOCK, DI), BF16), pltpu.VMEM((BLOCK, DI), BF16), pltpu.VMEM((BLOCK, DI), BF16),
            pltpu.VMEM((BLOCK, DI), BF16), pltpu.VMEM((NSTATE, DI), BF16), pltpu.VMEM((8, DI), F32),
            pltpu.VMEM((NSTATE, DI), BF16), pltpu.VMEM((T + 8, CH), F32), pltpu.VMEM((T + 16, CH), F32),
        ],
        compiler_params=params(),
        name="third_pass",
    )(act, convin, convin, halo, dt, cum, sig, dcum, mlow, ent, leave, egrad, rg, inc, rows, conv, head, et)


def from_behind(x, axis, by):
    peers = lax.axis_size(axis)
    pairs = [(i, i + by) for i in range(peers) if 0 <= i + by < peers]
    return lax.ppermute(x, axis, pairs)


def chain(total, leaving, axis, reverse):
    peers, index = lax.axis_size(axis), lax.axis_index(axis)
    decays = lax.all_gather(total, axis)
    states = lax.all_gather(leaving.astype(BF16), axis)
    acc = jnp.zeros(leaving.shape, F32)
    for k in range(peers):
        at = peers - 1 - k if reverse else k
        reached = (at > index) if reverse else (at < index)
        acc = jnp.where(reached, acc * decays[at] + states[at].astype(F32), acc)
    return acc


def pad_lanes(x, width):
    return jnp.pad(x, ((0, 0), (0, width - x.shape[1])))


def on_device(
    tokens, cotangent, norm_gain, in_weight, conv_weight, conv_bias, step_bias, decay_log, skip_gain, gate_gain,
    out_weight,
):
    both = ("dp", "seq")
    gather = functools.partial(lax.all_gather, axis_name=both, axis=0, tiled=True)
    w_in = gather(in_weight)
    wo = gather(out_weight)
    taps = gather(conv_weight)
    small = gather(norm_gain), gather(conv_bias), gather(gate_gain)
    tok, cot = tokens[0], cotangent[0]
    L = tok.shape[0]
    wg = w_in[:, :DI]
    wc = jnp.pad(w_in[:, DI:], ((0, 0), (0, DI + CH + BLOCK - w_in.shape[1])))
    gain = small[0].astype(F32)[None]
    conv = jnp.concatenate([taps.astype(F32).T, small[1].astype(F32)[None], jnp.zeros((3, CH), F32)], axis=0)
    head = pad_lanes(jnp.stack([step_bias, -jnp.exp(decay_log)] + [jnp.zeros_like(step_bias)] * 6), BLOCK)
    skip = jnp.repeat(skip_gain, HEADDIM)[None]
    rows = jnp.concatenate([small[2].astype(F32)[None], skip, jnp.zeros((6, DI), F32)], axis=0)
    et = jnp.asarray(head_columns(), BF16)

    halo = from_behind(tok[L - 16 :], "seq", 1)
    normed, convin, act, dt, cum, sig, bst, leave, tot = first_pass(tok, halo, wc, gain, conv, head)
    total = jnp.repeat(jnp.exp2(tot[0, :HEADS]), HEADDIM)[None]
    inc = chain(total, leave, "seq", False)
    mixed, nout, ggrad, mlow, dcum, ent, egrad, rg, leave2, back, cols = second_pass(
        normed, act, dt, cum, bst, inc, tok, cot, wg, wo, rows, et
    )
    g_out = lax.dot_general(nout, cot, (((0,), (0,)), ((), ())), preferred_element_type=F32)
    g_gate = lax.dot_general(normed, ggrad, (((0,), (0,)), ((), ())), preferred_element_type=F32)
    later = chain(total, back, "seq", True)
    halo_conv = from_behind(convin[L - 16 :], "seq", 1)
    pg, raw, cgrad, hgrad, gfirst, glast = third_pass(
        act, convin, halo_conv, dt, cum, sig, dcum, mlow, ent, leave2, egrad, rg, later, rows, conv, head, et
    )
    after = from_behind(gfirst, "seq", -1)
    fix = [sum(conv[k] * after[i - k] for k in range(i + 1)) for i in range(CONV - 1)]
    tail = glast[5:8] + jnp.stack(fix)
    pg = lax.dynamic_update_slice(pg, tail.astype(BF16), (L - 3, 0))
    g_conv = lax.dot_general(normed, pg, (((0,), (0,)), ((), ())), preferred_element_type=F32)
    g_step = lax.dot_general(normed, raw, (((0,), (0,)), ((), ())), preferred_element_type=F32)
    nig = dot_nt(ggrad, wg) + dot_nt(pg, wc[:, :CH]) + dot_nt(raw, wc[:, CH:])
    x = tok.astype(F32)
    inv = lax.rsqrt(jnp.mean(x * x, axis=-1, keepdims=True) + EPS)
    u = nig * gain
    tgrad = (cot.astype(F32) + inv * u - x * (inv**3 * jnp.mean(u * x, axis=-1, keepdims=True))).astype(BF16)
    norm_gain_grad = jnp.sum(nig * x * inv, axis=0)
    in_grad = jnp.concatenate([g_gate, g_conv, g_step[:, :HEADS]], axis=1)
    cg = cgrad.reshape(5, 8, CH).sum(axis=1)
    scatter = functools.partial(lax.psum_scatter, axis_name=both, scatter_dimension=0, tiled=True)
    hg = hgrad.reshape(2, 8, BLOCK).sum(axis=1)[:, :HEADS]
    gg = cols.reshape(2, 8, DI).sum(axis=1)
    sums = lax.psum((hg[0], hg[1], gg[1].reshape(HEADS, HEADDIM).sum(axis=1)), both)
    return (
        mixed[None], tgrad[None], scatter(norm_gain_grad), scatter(in_grad), scatter(cg[:4].T), scatter(cg[4]),
        sums[0], sums[1], sums[2], scatter(gg[0]), scatter(g_out),
    )


def solution(mesh):
    both = ("dp", "seq")
    vec, mat, tok, rep = P(both), P(both, None), P("dp", "seq", None), P()
    return jax.shard_map(
        on_device,
        mesh=mesh,
        in_specs=(tok, tok, vec, mat, mat, vec, rep, rep, rep, vec, mat),
        out_specs=(tok, tok, vec, mat, mat, vec, rep, rep, rep, vec, mat),
        check_vma=False,
    )
```

time: 1110 us -> 573 us (0.52)
  matrix products: 422 us -> 53.5 us
  other arithmetic: 280 us -> 27.3 us
  local copies, waits for them, and re-layouts: 192 us -> 22.3 us
  Pallas kernels: 0 us -> 169 us
  waiting for transfers between devices: 53.7 us -> 145 us
    dot_general x46 -> x7, matrix products: 422 us -> 53.5 us  [the longest x3 21.5 us: dot_nt(): return lax.dot_general(a, b, NT, preferred_element_type=F32)]
    pallas_call x0 -> x3, Pallas kernels: none -> 169 us  [the longest x1 76.2 us: third_pass(): pl.pallas_call(functools.partial(third_kernel, T), grid=(n,), in_specs=[r...]
    reduce_sum x11 -> x5, other arithmetic: 94.1 us -> 0.94 us  [the longest x1 0.68 us: on_device(): inv = lax.rsqrt(jnp.mean(x * x, axis=-1, keepdims=True) + EPS)]
    all_gather x4, waiting for transfers between devices: 0.06 us -> 62.1 us  [the longest x1 57.5 us: on_device(): wo = gather(out_weight)]
    unnamed x215 -> x42, local copies, waits for them, and re-layouts: 56.7 us -> 9.72 us
    another operation x7 -> x4, other arithmetic: 46.9 us -> 1.39 us  [the longest x2 1.39 us: on_device(): jnp.stack([step_bias, -jnp.exp(decay_log)] + [jnp.zeros_like(step_bias)]...]
    convert_element_type x18 -> x4, other arithmetic: 49.7 us -> 4.69 us  [the longest x2 3.83 us: chain(): states = lax.all_gather(leaving.astype(BF16), axis)]
    add x3 -> x0, local copies, waits for them, and re-layouts: 40.7 us -> none  [the longest x1 20.2 us: on_device(): mixed_f * skip_gain[:, None] + join_groups(values_part) + values_weight]
  transfers between devices with their start and end apart: 8 -> 9, of which waited for: 1 -> 4; matrix products, arithmetic and copies ran while one was open for 53% -> 17% of each run, Pallas kernels for 0% -> 13%
where the time goes in v1:
time: 573 us; the launch traced here: 567 us
  Pallas kernels  169 us (29%)
  waiting for transfers between devices  145 us (25%)
  blocking collectives  129 us (23%)
  matrix products  53.5 us (9%)
  other arithmetic  27.3 us (5%)
  local copies, waits for them, and re-layouts  22.3 us (4%)
  between operations  14.9 us (3%)
  starting transfers between devices  6.03 us (1%)
    unnamed x2, blocking collectives  83.1 us
    unnamed x7, waiting for transfers between devices  81.9 us
    pallas_call x1, Pallas kernels, third_pass(): pl.pallas_call(functools.partial(third_kernel, T), grid=(n,), in_specs=[r...  76.2 us
    pallas_call x1, Pallas kernels, second_pass(): pl.pallas_call(functools.partial(second_kernel, T), grid=(L // T,), in_sp...  57.6 us
    all_gather x1, waiting for transfers between devices, on_device(): wo = gather(out_weight)  57.5 us
    all_gather x1, blocking collectives, on_device(): taps = gather(conv_weight)  40.6 us
    pallas_call x1, Pallas kernels, first_pass(): pl.pallas_call(functools.partial(first_kernel, T), grid=(L // T,), in_spe...  35.6 us
    dot_general x3, matrix products, dot_nt(): return lax.dot_general(a, b, NT, preferred_element_type=F32)  21.5 us
  transfers between devices with their start and end apart: 9, of which 4 were waited for; matrix products, arithmetic and copies ran while one was open for 17% of the time, Pallas kernels for 13%

profile of v1, /device:TPU:0, one launch (start us, length us, event | category | flops | bytes accessed | tf_op | source)
XLA Modules:
  0.0 567.3 jit_solution(13949266224152085378)
XLA Ops:
  7.2 0.7 all-gather.8.cloned.1.call-update
  8.0 0.7 slice_bitcast_fusion.1
  8.7 2.3 collective-permute-start
  11.1 0.9 dynamic-update-slice.1
  11.9 0.8 dynamic-update-slice.2
  12.8 0.8 dynamic-update-slice
  13.6 42.1 %all-reduce.11 = (bf16[768]{0:T(1024)(128)(2,1)S(1)}, bf16[1792]{0:T(1024)(128)(2,1)S(1)}, bf16[1536]{0:T(1024)(128)(2,1)S(1)}) all-reduce(bf16[768]{0:T(1024)(128)(2,1)S(1)} %dynamic-update-slice, bf16[1792]{0:T(1024)(128)(2,1)S(1)} %dynamic-update-slice.1, ...), channel_id=1, replica_groups=mesh['dp'=8,'seq'=4] {'dp','seq'}, use_global_device_ids=true, to_apply=%add.2 | all-reduce | flops 4096 | bytes 16384
  55.7 40.6 %all-gather.2 = bf16[32,56,4]{1,2,0:T(4,128)(2,1)S(1)} all-gather(bf16[1,56,4]{1,2,0:T(4,128)(2,1)} %bitcast.53), channel_id=1, replica_groups=mesh['dp'=8,'seq'=4] {'dp','seq'}, dimensions={0}, use_global_device_ids=true | all-gather | bytes 14784 | tf_op jit(solution)/shard_map/all_gather | solution.py:491
  96.7 0.7 negate_bitcast_fusion
  97.3 0.7 maximum_maximum_fusion.conv_ref
  98.0 0.7 maximum_maximum_fusion.2
  99.9 2.0 slice.160
  102.0 1.6 copy-done.1
  103.6 1.8 pad.8.wc_ref
  106.0 35.6 %first_pass.1 = (bf16[2048,768]{1,0:T(8,128)(2,1)}, bf16[2048,1792]{1,0:T(8,128)(2,1)}, bf16[2048,1792]{1,0:T(8,128)(2,1)}, f32[2048,128]{1,0:T(8,128)}, f32[204...) custom-call(bf16[2048,768]{1,0:T(8,128)(2,1)} %bitcast.46, ...), custom_call_target="tpu_custom_call" | custom-call | tf_op jit(solution)/shard_map/first_pass/pallas_call | solution.py:381
  141.6 1.9 convert_element_type.77
  143.6 0.7 all-gather.10.cloned.1.call-update
  144.6 0.7 maximum_maximum_fusion.1.row_ref
  145.3 0.7 exponential_bitcast_fusion
  146.1 3.4 slice.169.wg_ref
  149.5 5.4 all_gather.38
  155.0 4.6 all-gather.12.cloned.1.call-done
  159.6 2.6 fusion.14.inc_ref
  162.3 57.5 %all-gather.10.cloned.1.call-done.wo_ref = bf16[1536,768]{1,0:T(8,128)(2,1)} async-done(((bf16[48,768]{1,0:T(8,128)(2,1)}), bf16[1536,768]{1,0:T(8,128)(2,1)}) %all-gather.10.cloned.1.call-update) | async-done | bytes 2359312 | tf_op jit(solution)/shard_map/all_gather | solution.py:490
  219.7 57.6 %second_pass.1 = (bf16[2048,768]{1,0:T(8,128)(2,1)}, bf16[2048,1536]{1,0:T(8,128)(2,1)}, bf16[2048,1536]{1,0:T(8,128)(2,1)}, bf16[2048,1536]{1,0:T(8,128)(2,1)},...) custom-call(bf16[2048,768]{1,0:T(8,128)(2,1)} %get-tuple-element.37., ...), custom_call_target="tpu_custom_call" | custom-call | tf_op jit(solution)/shard_map/second_pass/pallas_call | solution.py:406
  277.3 1.9 convert_element_type.88
  279.3 8.7 %fusion.26 = f32[1536,768]{1,0:T(8,128)} fusion(bf16[2048,1536]{1,0:T(8,128)(2,1)} %get-tuple-element.62, bf16[1,2048,768]{2,1,0:T(8,128)(2,1)S(1)} %copy-done.3), kind=kOutput, calls=%fused_computation.70 | convolution fusion | flops 4831838208 | bytes 14155776 | tf_op jit(solution)/shard_map/dot_general | solution.py:511
  288.1 0.8 slice.130
  288.9 2.2 collective-permute-start.1
  291.1 9.7 %fusion.31 = f32[768,1536]{1,0:T(8,128)} fusion(bf16[2048,768]{1,0:T(8,128)(2,1)} %get-tuple-element.37.normed_ref, bf16[2048,1536]{1,0:T(8,128)(2,1)} %get-tuple-element.45), kind=kOutput, calls=%fused_computation.75 | convolution fusion | flops 4831838208 | bytes 14155776 | tf_op jit(solution)/shard_map/dot_general | solution.py:512
  300.8 2.6 fusion.9.inc_ref
  304.0 76.2 %third_pass.1 = (bf16[2048,1792]{1,0:T(8,128)(2,1)}, bf16[2048,128]{1,0:T(8,128)(2,1)}, f32[40,1792]{1,0:T(8,128)}, f32[16,128]{1,0:T(8,128)}, f32[8,1792]{1,0:T(8,128)}, /*index=5*/f32[8,1792]{1,0:T(8,128)}) custom-call(bf16[2048,1792]{1,0:T(8,128)(2,1)} %get-tuple-element.38.act_ref, bf16[2048,1792]{1,0:T(8,128)(2,1)} %get-tuple-element.46.convin_ref.prev_ref, ...), custom_call_target="tpu_custom_call" | custom-call | tf_op jit(solution)/shard_map/third_pass/pallas_call | solution.py:438
  380.2 1.3 collective-permute-start.2
  381.5 2.1 fusion.19
  383.7 0.7 collective-permute-done.2
  384.4 0.9 fusion.22
  385.3 1.6 dynamic_update_slice.3
  386.9 11.5 %fusion.32 = f32[768,1792]{1,0:T(8,128)} fusion(bf16[2048,768]{1,0:T(8,128)(2,1)} %get-tuple-element.37.normed_ref, bf16[2048,1792]{1,0:T(8,128)(2,1)} %dynamic_update_slice.3), kind=kOutput, calls=%fused_computation.76 | convolution fusion | flops 5637144576 | bytes 15990784 | tf_op jit(solution)/shard_map/dot_general | solution.py:522
  398.5 7.2 %pad_maximum_fusion = f32[768,3352]{1,0:T(8,128)} fusion(f32[768,24]{1,0:T(8,128)S(1)} %fusion.19, f32[768,1792]{1,0:T(8,128)} %fusion.32, f32[768,1536]{1,0:T(8,128)S(1)} %bitcast.50), kind=kLoop, calls=%fused_computation.4 | loop fusion | flops 5148672 | bytes 20594688 | tf_op jit(solution)/shard_map/concatenate | solution.py:530
  405.7 0.7 copy-done.11
  406.4 1.3 copy-done
  407.6 0.7 fusion
  408.6 8.0 %fusion.28 = f32[2048,768]{1,0:T(8,128)S(1)} fusion(bf16[2048,1536]{1,0:T(8,128)(2,1)} %get-tuple-element.45, bf16[768,3352]{1,0:T(8,128)(2,1)} %all-gather.8.cloned.1.call-done), kind=kOutput, calls=%fused_computation.72 | convolution fusion | flops 4831838208 | bytes 14942208 | tf_op jit(solution)/shard_map/dot_general | solution.py:33
  416.8 9.2 %fusion.7 = f32[2048,768]{1,0:T(8,128)S(1)} fusion(bf16[2048,1792]{1,0:T(8,128)(2,1)} %dynamic_update_slice.3, bf16[768,3352]{1,0:T(8,128)(2,1)} %all-gather.8.cloned.1.call-done), kind=kOutput, calls=%fused_computation.13 | convolution fusion | flops 5637144576 | bytes 16384000 | tf_op jit(solution)/shard_map/dot_general | solution.py:33
  426.0 4.4 fusion.5
  430.4 41.1 %all-reduce.10 = (f32[768]{0:T(1024)S(1)}, f32[1792,4]{0,1:T(4,128)S(1)}, f32[1792]{0:T(1024)S(1)}, f32[24]{0:T(128)}, f32[24]{0:T(128)}, /*index=5*/f32[24]{0:T(128)}, f32[1536]{0:T(1024)S(1)}) all-reduce(f32[768]{0:T(1024)S(1)} %get-tuple-element.63, ...), channel_id=4, replica_groups=mesh['dp'=8,'seq'=4] {'dp','seq'}, use_global_device_ids=true, to_apply=%region_3.4.clone | all-reduce | flops 11336 | bytes 90688
  473.9 5.7 %fusion.6 = bf16[1,2048,768]{2,1,0:T(8,128)(2,1)} fusion(f32[2048,768]{1,0:T(8,128)} %get-tuple-element.86, f32[2048]{0:T(1024)S(1)} %fusion.23, f32[768]{0:T(1024)S(1)} %convert_element_type.76, f32[2048]{0:T(1024)S(1)} %add_rsqrt_fusion, bf16[1,2048,768]{2,1,0:T(8,128)(2,1)} %param.13, bf16[1,2048,768]{2,1,0:T(8,128)(2,1)S(1)} %copy-done), kind=kLoop, calls=%fused_computation.12 | loop fusion | flops 12582912 | bytes 15748096 | tf_op jit(solution)/shard_map/broadcast_in_dim | solution.py:537
  479.6 80.4 %reduce-scatter.8.cloned.1.call-done = f32[24,3352]{1,0:T(8,128)} async-done(((f32[768,3352]{1,0:T(8,128)}), f32[24,3352]{1,0:T(8,128)}) %reduce-scatter.8.cloned.1.call-update) | async-done | bytes 321808
  (86 shorter events, 6.5 us)
Async XLA Ops:
  7.2 92.8 %all-gather.8.cloned.1.call-start = ((), (), s32[]{:S(2)}) async-start(), calls=%async_computation.2 | async-start | bytes 5474304 | tf_op jit(solution)/shard_map/all_gather | solution.py:489
  7.9 151.7 %all-gather.12.cloned.1.call-start = ((), (), s32[]{:S(2)}) async-start(), calls=%async_computation.5 | async-start | bytes 1966080 | tf_op jit(solution)/shard_map/all_gather | solution.py:470
  8.7 96.7 %collective-permute-start = (bf16[16,768]{1,0:T(8,128)(2,1)S(1)}, bf16[16,768]{1,0:T(8,128)(2,1)S(1)}, u32[]{:S(2)}, u32[]{:S(2)}) collective-permute-start(bf16[16,768]{1,0:T(8,128)(2,1)S(1)} %slice_bitcast_fusion.1), channel_id=1, source_target_pairs={{0,1},{1,2},{2,3},{4,5},{5,6},{6,7},{8,9},{9,10},{10,11},{12,13},{... | collective-permute-start | bytes 73736 | tf_op jit(solution)/shard_map/ppermute | solution.py:464
  55.7 85.9 %copy-start.10 = (bf16[768]{0:T(1024)(128)(2,1)}, bf16[768]{0:T(1024)(128)(2,1)S(1)}, u32[]{:S(2)}) copy-start(bf16[768]{0:T(1024)(128)(2,1)S(1)} %get-tuple-element.78) | copy-start | bytes 4612
  102.0 1.6 copy-start.1
  103.6 40.8 %copy-start.13 = (f32[24]{0:T(128)S(1)}, f32[24]{0:T(128)}, u32[]{:S(2)}) copy-start(f32[24]{0:T(128)} %param.20) | copy-start | bytes 292
  105.4 0.6 copy-start.9
  143.6 76.2 %all-gather.10.cloned.1.call-start = ((), (), s32[]{:S(2)}) async-start(), calls=%async_computation.3 | async-start | bytes 2433024 | tf_op jit(solution)/shard_map/all_gather | solution.py:490
  144.3 156.5 %all-gather.14.cloned.1.call-start = ((), (), s32[]{:S(2)}) async-start(), calls=%async_computation.6 | async-start | bytes 1966080 | tf_op jit(solution)/shard_map/all_gather | solution.py:470
  219.7 59.6 %copy-start.3 = (bf16[1,2048,768]{2,1,0:T(8,128)(2,1)S(1)}, bf16[1,2048,768]{2,1,0:T(8,128)(2,1)}, u32[]{:S(2)}) copy-start(bf16[1,2048,768]{2,1,0:T(8,128)(2,1)} %param.13) | copy-start | bytes 9437188
  279.3 200.3 %reduce-scatter.6.cloned.1.call-start = ((), (), s32[]{:S(2)}) async-start(), calls=%async_computation.4 | async-start | bytes 4866048 | tf_op jit(solution)/shard_map/reduce_scatter | solution.py:538
  288.0 272.0 %reduce-scatter.8.cloned.1.call-start = ((), (), s32[]{:S(2)}) async-start(), calls=%async_computation.7 | async-start | bytes 10948608
  288.9 14.5 %collective-permute-start.1 = (bf16[16,1792]{1,0:T(8,128)(2,1)S(1)}, bf16[16,1792]{1,0:T(8,128)(2,1)S(1)}, u32[]{:S(2)}, u32[]{:S(2)}) collective-permute-start(bf16[16,1792]{1,0:T(8,128)(2,1)S(1)} %slice.130), channel_id=1, source_target_pairs={{0,1},{1,2},{2,3},{4,5},{5,6},{6,7},{8,9},{9,10},{10,11},{12,13},{... | collective-permute-start | bytes 172040 | tf_op jit(solution)/shard_map/ppermute | solution.py:464
  303.4 0.6 copy-start.8
  304.0 77.5 %copy-start.4 = (bf16[2048,768]{1,0:T(8,128)(2,1)S(1)}, bf16[2048,768]{1,0:T(8,128)(2,1)}, u32[]{:S(2)}) copy-start(bf16[2048,768]{1,0:T(8,128)(2,1)} %get-tuple-element.37.normed_ref) | copy-start | bytes 9437188
  380.2 4.2 collective-permute-start.2
  381.5 16.9 %slice-start = ((s8[4718592]{0:T(1024)(128)(4,1)}), s8[524288]{0:T(1024)(128)(4,1)S(1)}, s32[]{:S(2)}) async-start(s8[4718592]{0:T(1024)(128)(4,1)} %bitcast.49), calls=%async_computation.8 | async-start | bytes 1048576
  386.9 11.5 %slice-start.1 = ((s8[4718592]{0:T(1024)(128)(4,1)}), s8[4194304]{0:T(1024)(128)(4,1)S(1)}, s32[]{:S(2)}) async-start(s8[4718592]{0:T(1024)(128)(4,1)} %bitcast.49), calls=%async_computation.9 | async-start | bytes 8388608
  405.7 0.7 copy-start.11
  405.7 1.9 copy-start
  405.7 2.6 copy-start.7
  408.6 8.0 %copy-start.12 = (f32[16,128]{1,0:T(8,128)S(1)}, f32[16,128]{1,0:T(8,128)}, u32[]{:S(2)}) copy-start(f32[16,128]{1,0:T(8,128)} %get-tuple-element.60) | copy-start | bytes 24580
  408.6 8.0 %copy-start.6 = (f32[40,1792]{1,0:T(8,128)S(1)}, f32[40,1792]{1,0:T(8,128)}, u32[]{:S(2)}) copy-start(f32[40,1792]{1,0:T(8,128)} %get-tuple-element.59) | copy-start | bytes 860164
  416.8 9.2 %copy-start.2 = (bf16[768,1816]{1,0:T(8,128)(2,1)S(1)}, bf16[768,1816]{1,0:T(8,128)(2,1)}, u32[]{:S(2)}) copy-start(bf16[768,1816]{1,0:T(8,128)(2,1)} %copy-done.1) | copy-start | bytes 8368132
  416.8 9.2 %copy-start.5 = (bf16[2048,128]{1,0:T(8,128)(2,1)S(1)}, bf16[2048,128]{1,0:T(8,128)(2,1)}, u32[]{:S(2)}) copy-start(bf16[2048,128]{1,0:T(8,128)(2,1)} %get-tuple-element.58) | copy-start | bytes 1572868
Sparse Core Ops, SparseCore 0:
  10.8 68.4 all-gather.7
  143.7 15.9 all-gather.11
  162.6 57.1 all-gather.9
  279.4 18.5 all-gather.13
  303.9 107.5 reduce-scatter.5
  419.0 140.9 reduce-scatter.7

commit v2 on v1

--- a/solution.py
+++ b/solution.py
@@ -66,6 +66,544 @@
     return slice(j * BLOCK, (j + 1) * BLOCK)
 
 
+MESH = pl.DeviceIdType.MESH
+ANY = pl.BlockSpec(memory_space=pl.ANY)
+WC = CH + BLOCK
+TN = (((0,), (0,)), ((), ()))
+
+
+def dot_tn(a, b):
+    return lax.dot_general(a, b, TN, preferred_element_type=F32)
+
+
+def sizes():
+    return {"z": lax.axis_size("dp") // 2, "x": 2, "y": lax.axis_size("seq") // 2, "c": 2}
+
+
+def place():
+    dp, seq = lax.axis_index("dp"), lax.axis_index("seq")
+    return {"z": dp // 2, "x": lax.rem(dp, 2), "y": seq // 2, "c": lax.rem(seq, 2)}
+
+
+def device(at):
+    return {"dp": at["z"] * 2 + at["x"], "seq": at["y"] * 2 + at["c"]}
+
+
+def peers(at, axis):
+    n = sizes()[axis]
+    return [dict(at, **{axis: lax.rem(at[axis] + o, n)}) for o in range(1, n)]
+
+
+def greet(at, axes, by=0):
+    sem = pltpu.get_barrier_semaphore()
+    count = 0
+    for axis in axes:
+        for peer in peers(at, axis):
+            pl.semaphore_signal(sem, inc=1, device_id=device(peer), device_id_type=MESH)
+            count += 1
+    if not by:
+        pl.semaphore_wait(sem, count)
+        return
+    seq, n = lax.axis_index("seq"), lax.axis_size("seq")
+
+    @pl.when((seq + by >= 0) & (seq + by < n))
+    def _():
+        pl.semaphore_signal(sem, inc=1, device_id={"seq": seq + by}, device_id_type=MESH)
+
+    heard = (seq - by >= 0) & (seq - by < n)
+
+    @pl.when(heard)
+    def _():
+        pl.semaphore_wait(sem, count + 1)
+
+    @pl.when(jnp.logical_not(heard))
+    def _():
+        pl.semaphore_wait(sem, count)
+
+
+def greet_neighbours():
+    seq, n = lax.axis_index("seq"), lax.axis_size("seq")
+    sem = pltpu.get_barrier_semaphore()
+
+    @pl.when(seq > 0)
+    def _():
+        pl.semaphore_signal(sem, inc=1, device_id={"seq": seq - 1}, device_id_type=MESH)
+
+    @pl.when(seq < n - 1)
+    def _():
+        pl.semaphore_signal(sem, inc=1, device_id={"seq": seq + 1}, device_id_type=MESH)
+
+    @pl.when((seq > 0) & (seq < n - 1))
+    def _():
+        pl.semaphore_wait(sem, 2)
+
+    @pl.when((seq == 0) | (seq == n - 1))
+    def _():
+        pl.semaphore_wait(sem, 1)
+
+
+def remote(src, dst, send, recv, peer):
+    return pltpu.make_async_remote_copy(
+        src_ref=src, dst_ref=dst, send_sem=send, recv_sem=recv, device_id=device(peer), device_id_type=MESH
+    )
+
+
+class Gather:
+    def __init__(self, slab, buf, order, sems, lanes=slice(None)):
+        self.slab, self.buf, self.order, self.lanes = slab, buf, order, lanes
+        self.send, self.recv, self.local = sems
+        self.at = place()
+        self.count = 0
+
+    def spot(self, index):
+        return self.buf.at[index["z"], index["x"], index["y"], index["c"], :, self.lanes]
+
+    def copies(self, stage):
+        at, (a, b) = self.at, self.order
+        n = sizes()
+        out = []
+        every = slice(None)
+        nz = n["z"] - 1
+        if stage == 0:
+            src, dst = self.slab.at[:, self.lanes], self.spot(at)
+            for o, peer in enumerate(peers(at, "z")):
+                out.append((src, dst, o, peer))
+        elif stage == 1:
+            index = dict(at, z=every)
+            out.append((self.spot(index), self.spot(index), nz, peers(at, a)[0]))
+        elif stage == 2:
+            index = dict(at, z=every)
+            index[a] = every
+            for o, peer in enumerate(peers(at, b)):
+                out.append((self.spot(index), self.spot(index), nz + 1 + o, peer))
+            out.append((self.spot(index), self.spot(index), nz + 1 + n[b] - 1, peers(at, "c")[0]))
+        else:
+            for o in range(1, n[b]):
+                index = dict(at, z=every)
+                index[a] = every
+                index[b] = lax.rem(at[b] + o, n[b])
+                out.append((self.spot(index), self.spot(index), nz + 1 + n[b] + o - 1, peers(at, "c")[0]))
+        return [remote(s, d, self.send.at[k], self.recv.at[k], p) for s, d, k, p in out]
+
+    def own(self):
+        return pltpu.make_async_copy(self.slab.at[:, self.lanes], self.spot(self.at), self.local)
+
+    def start(self, stage):
+        if stage == 0:
+            self.own().start()
+        for c in self.copies(stage):
+            c.start()
+
+    def wait(self, stage):
+        for c in self.copies(stage):
+            c.wait()
+        if stage == 0:
+            self.own().wait()
+
+
+def gather_sems():
+    count = sizes()["z"] + 2 * sizes()["y"] + 4
+    return [pltpu.SemaphoreType.DMA((count,)), pltpu.SemaphoreType.DMA((count,)), pltpu.SemaphoreType.DMA(())]
+
+
+class Scatter:
+    def __init__(self, grads, out, order, scratch):
+        self.grads, self.out, self.order = grads, out, order
+        self.own, self.rc, self.r1, self.r2, self.rz, self.send, self.recv, self.local = scratch
+        self.at = place()
+
+    def copies(self, stage):
+        at, (a, b) = self.at, self.order
+        every = slice(None)
+        out = []
+
+        def spot(index):
+            return self.own.at[index["z"], index["x"], index["y"]]
+
+        if stage == 0:
+            out.append((self.grads.at[:, :, :, 1 - at["c"]], self.rc, 0, peers(at, "c")[0]))
+        elif stage == 1:
+            index = {"z": every, "x": every, "y": every}
+            index[a] = 1 - at[a]
+            out.append((spot(index), self.r1, 1, peers(at, a)[0]))
+        elif stage == 2:
+            index = {"z": every, a: at[a], b: 1 - at[b]}
+            out.append((spot(index), self.r2, 2, peers(at, b)[0]))
+        else:
+            for o, peer in enumerate(peers(at, "z")):
+                out.append((self.own.at[peer["z"], at["x"], at["y"]], self.rz.at[o], 3 + o, peer))
+        return [remote(s, d, self.send.at[k], self.recv.at[k], p) for s, d, k, p in out]
+
+    def mine(self):
+        return pltpu.make_async_copy(self.grads.at[:, :, :, self.at["c"]], self.own, self.local)
+
+    def start(self, stage):
+        if stage == 0:
+            self.mine().start()
+        for c in self.copies(stage):
+            c.start()
+
+    def finish(self, stage):
+        at, (a, b) = self.at, self.order
+        for c in self.copies(stage):
+            c.wait()
+        nz = sizes()["z"]
+
+        def add(x, y):
+            return (x.astype(F32) + y.astype(F32)).astype(BF16)
+
+        if stage == 0:
+            self.mine().wait()
+
+            def body(z, _):
+                for x in range(2):
+                    for y in range(2):
+                        self.own[z, x, y] = add(self.own[z, x, y], self.rc[z, x, y])
+                return _
+
+            lax.fori_loop(0, nz, body, 0)
+        elif stage == 1:
+
+            def body(z, _):
+                for k in range(2):
+                    index = {a: at[a], b: k}
+                    got = self.own[z, index["x"], index["y"]]
+                    self.own[z, index["x"], index["y"]] = add(got, self.r1[z, k])
+                return _
+
+            lax.fori_loop(0, nz, body, 0)
+        elif stage == 2:
+
+            def body(z, _):
+                self.own[z, at["x"], at["y"]] = add(self.own[z, at["x"], at["y"]], self.r2[z])
+                return _
+
+            lax.fori_loop(0, nz, body, 0)
+        else:
+            total = self.own[at["z"], at["x"], at["y"]].astype(F32)
+            for o in range(nz - 1):
+                total = total + self.rz[o].astype(F32)
+            self.out[...] = total
+
+
+def scatter_scratch(rows, width):
+    nz = sizes()["z"]
+    return [
+        pltpu.VMEM((nz, 2, 2, rows, width), BF16), pltpu.VMEM((nz, 2, 2, rows, width), BF16),
+        pltpu.VMEM((nz, 2, rows, width), BF16), pltpu.VMEM((nz, rows, width), BF16),
+        pltpu.VMEM((nz - 1, rows, width), BF16), pltpu.SemaphoreType.DMA((nz + 2,)), pltpu.SemaphoreType.DMA((nz + 2,)),
+        pltpu.SemaphoreType.DMA(()),
+    ]
+
+
+NSC = 8
+
+
+class Chain:
+    def __init__(self, leave, inc, decay, bufs, reverse):
+        self.leave, self.inc, self.decay, self.reverse = leave, inc, decay, reverse
+        self.got, self.put, self.send, self.recv = bufs
+        self.n = lax.axis_size("seq")
+        seq = lax.axis_index("seq")
+        self.rank = self.n - 1 - seq if reverse else seq
+        self.to = seq - 1 if reverse else seq + 1
+
+    def copy(self):
+        return pltpu.make_async_remote_copy(
+            src_ref=self.put, dst_ref=self.got, send_sem=self.send, recv_sem=self.recv,
+            device_id={"seq": self.to}, device_id_type=MESH,
+        )
+
+    def step(self, k):
+        @pl.when(self.rank == k)
+        def _():
+            if k == 0:
+                self.inc[...] = jnp.zeros_like(self.inc)
+                self.put[...] = self.leave[...].astype(BF16)
+            else:
+                self.copy().wait_recv()
+                got = self.got[...].astype(F32)
+                self.inc[...] = got
+                if k < self.n - 1:
+                    self.put[...] = (got * self.decay[0:1] + self.leave[...]).astype(BF16)
+            if k < self.n - 1:
+                self.copy().start()
+
+    def done(self):
+        @pl.when(self.rank < self.n - 1)
+        def _():
+            self.copy().wait_send()
+
+
+def chain_scratch():
+    return [
+        pltpu.VMEM((NSTATE, DI), BF16), pltpu.VMEM((NSTATE, DI), BF16), pltpu.SemaphoreType.DMA(()),
+        pltpu.SemaphoreType.DMA(()),
+    ]
+
+
+def expand_row(row, dst):
+    lo = iota((8, BLOCK), 1) < HEADDIM
+    wide = jnp.broadcast_to(row, (8, BLOCK))
+    for j in range(PAIRS):
+        dst[:, pair(j)] = expand_pair(wide, j, lo)[0]
+
+
+def weights_kernel(slab, last, buf, halo, *sems):
+    at = place()
+    seq, n = lax.axis_index("seq"), lax.axis_size("seq")
+    greet(at, "zxyc", -1)
+    hsend, hrecv = sems[6], sems[7]
+    copy = pltpu.make_async_remote_copy(
+        src_ref=last, dst_ref=halo, send_sem=hsend, recv_sem=hrecv, device_id={"seq": seq + 1}, device_id_type=MESH
+    )
+    a = Gather(slab, buf, "xy", sems[0:3], slice(0, 1024))
+    b = Gather(slab, buf, "yx", sems[3:6], slice(1024, WC))
+    a.start(0)
+    b.start(0)
+
+    @pl.when(seq < n - 1)
+    def _():
+        copy.start()
+
+    for stage in range(3):
+        a.wait(stage)
+        a.start(stage + 1)
+        b.wait(stage)
+        b.start(stage + 1)
+    a.wait(3)
+    b.wait(3)
+
+    @pl.when(seq < n - 1)
+    def _():
+        copy.wait_send()
+
+    @pl.when(seq > 0)
+    def _():
+        copy.wait_recv()
+
+    @pl.when(seq == 0)
+    def _():
+        halo[...] = jnp.zeros_like(halo)
+
+
+def gather_weights(slab, last):
+    n = sizes()
+    shape = (n["z"], n["x"], n["y"], n["c"]) + slab.shape
+    vm = pl.BlockSpec(memory_space=pltpu.VMEM)
+    return pl.pallas_call(
+        weights_kernel,
+        in_specs=[ANY, vm],
+        out_specs=[ANY, vm],
+        out_shape=[sds(shape, BF16), sds(last.shape, BF16)],
+        scratch_shapes=gather_sems() + gather_sems() + [pltpu.SemaphoreType.DMA(()), pltpu.SemaphoreType.DMA(())],
+        compiler_params=pltpu.CompilerParams(collective_id=0, has_side_effects=True),
+        name="gather_weights",
+    )(slab, last)
+
+
+def gate_kernel(normed_ref, wg_ref, leave_ref, tot_ref, gate_ref, inc_ref, decay, *bufs):
+    i = pl.program_id(0)
+    chain = Chain(leave_ref, inc_ref, decay, bufs, False)
+    last = pl.num_programs(0) - 1
+
+    @pl.when(i == 0)
+    def _():
+        expand_row(jnp.exp2(tot_ref[0:1]), decay)
+        greet_neighbours()
+        chain.step(0)
+
+    for c in range(DI // 256):
+        cs = slice(c * 256, (c + 1) * 256)
+        gate_ref[:, cs] = dot(normed_ref[...], wg_ref[:, cs]).astype(BF16)
+    for k in range(1, chain.n):
+        @pl.when(i == jnp.minimum(k, last))
+        def _():
+            chain.step(k)
+
+    @pl.when(i == last)
+    def _():
+        chain.done()
+
+
+def gate_pass(normed, wg, leave, tot, T=512):
+    L = normed.shape[0]
+    row = lambda w: pl.BlockSpec((T, w), lambda i: (i, 0))
+    return pl.pallas_call(
+        gate_kernel,
+        grid=(L // T,),
+        in_specs=[row(D), full((D, DI)), full((NSTATE, DI)), full((8, BLOCK))],
+        out_specs=[row(DI), full((NSTATE, DI))],
+        out_shape=[sds((L, DI), BF16), sds((NSTATE, DI), F32)],
+        scratch_shapes=[pltpu.VMEM((8, DI), F32)] + chain_scratch(),
+        compiler_params=params(collective_id=2),
+        name="gate_pass",
+    )(normed, wg, leave, tot)
+
+
+def grads_kernel(nout_ref, cot_ref, normed_ref, ggrad_ref, back_ref, tot_ref, gout_ref, ggate_ref, inc_ref, decay, *bufs):
+    i = pl.program_id(0)
+    chain = Chain(back_ref, inc_ref, decay, bufs, True)
+    last = pl.num_programs(0) - 1
+
+    @pl.when(i == 0)
+    def _():
+        expand_row(jnp.exp2(tot_ref[0:1]), decay)
+        greet_neighbours()
+        chain.step(0)
+
+    gout_ref[...] = dot_tn(nout_ref[...], cot_ref[...]).astype(BF16)
+    ggate_ref[...] = dot_tn(normed_ref[...], ggrad_ref[...]).astype(BF16)
+    for k in range(1, chain.n):
+        @pl.when(i == jnp.minimum(k, last))
+        def _():
+            chain.step(k)
+
+    @pl.when(i == last)
+    def _():
+        chain.done()
+
+
+def grads_pass(nout, cot, normed, ggrad, back, tot):
+    L = nout.shape[0]
+    col = lambda w: pl.BlockSpec((L, w), lambda i: (0, i))
+    return pl.pallas_call(
+        grads_kernel,
+        grid=(6,),
+        in_specs=[col(256), full((L, D)), col(128), full((L, DI)), full((NSTATE, DI)), full((8, BLOCK))],
+        out_specs=[
+            pl.BlockSpec((256, D), lambda i: (i, 0)), pl.BlockSpec((128, DI), lambda i: (i, 0)), full((NSTATE, DI)),
+        ],
+        out_shape=[sds((DI, D), BF16), sds((D, DI), BF16), sds((NSTATE, DI), F32)],
+        scratch_shapes=[pltpu.VMEM((8, DI), F32)] + chain_scratch(),
+        compiler_params=params(collective_id=3),
+        name="grads_pass",
+    )(nout, cot, normed, ggrad, back, tot)
+
+
+def conv_grad_kernel(normed_ref, pg_ref, tnormed_ref, tail_ref, out_ref):
+    for c in range(WC // 384):
+        cs = slice(c * 384, (c + 1) * 384)
+        g = dot_tn(normed_ref[...], pg_ref[:, cs])
+        out_ref[:, cs] = (g + dot_tn(tnormed_ref[...], tail_ref[:, cs])).astype(BF16)
+
+
+def conv_grad(normed, pg, tail):
+    L = normed.shape[0]
+    return pl.pallas_call(
+        conv_grad_kernel,
+        grid=(3,),
+        in_specs=[
+            pl.BlockSpec((L, 256), lambda i: (0, i)), full((L, WC)), pl.BlockSpec((16, 256), lambda i: (L // 16 - 1, i)),
+            full((16, WC)),
+        ],
+        out_specs=pl.BlockSpec((256, WC), lambda i: (i, 0)),
+        out_shape=sds((D, WC), BF16),
+        compiler_params=params(),
+        name="conv_grad",
+    )(normed, pg, normed, tail)
+
+
+def last_kernel(
+    T, ggrad_ref, pg_ref, tail_ref, tok_ref, cot_ref, wg_ref, wc_ref, gain_ref, small_ref, gconv_ref,
+    tgrad_ref, gout_ref, sums_ref, ngain, packed, smalls, ssend, srecv, *scratch,
+):
+    i = pl.program_id(0)
+    last = pl.num_programs(0) - 1
+    at = place()
+    sc = Scatter(gconv_ref, gout_ref, "yx", scratch)
+    dp, seq = lax.axis_index("dp"), lax.axis_index("seq")
+    n_dp, n_seq = lax.axis_size("dp"), lax.axis_size("seq")
+    total = n_dp * n_seq
+    me = dp * n_seq + seq
+
+    def far(o):
+        r = lax.rem(me + o, total)
+        return r, {"dp": r // n_seq, "seq": lax.rem(r, n_seq)}
+
+    @pl.when(i == 0)
+    def _():
+        ngain[...] = jnp.zeros_like(ngain)
+        sem = pltpu.get_barrier_semaphore()
+        for o in range(1, total):
+            pl.semaphore_signal(sem, inc=1, device_id=far(o)[1], device_id_type=MESH)
+        pl.semaphore_wait(sem, total - 1)
+        sc.start(0)
+
+    def part():
+        nig = dot_nt(ggrad_ref[...], wg_ref[...]) + dot_nt(pg_ref[...], wc_ref[...])
+        return nig
+
+    x = tok_ref[...].astype(F32)
+    inv = lax.rsqrt(jnp.mean(x * x, axis=-1, keepdims=True) + EPS)
+    nig = part()
+    fix = dot_nt(tail_ref[...], wc_ref[...])
+    fix = jnp.where(i == last, fix, 0.0)
+    nig = jnp.concatenate([nig[: T - 16], nig[T - 16 :] + fix], axis=0)
+    u = nig * gain_ref[...]
+    xi = x * inv
+    coef = inv * jnp.mean(u * xi, axis=-1, keepdims=True)
+    tgrad_ref[...] = (cot_ref[...].astype(F32) + inv * u - xi * coef).astype(BF16)
+    ngain[...] += jnp.sum((nig * xi).reshape(T // 8, 8, D), axis=0)
+
+    for k in range(3):
+        @pl.when(i == jnp.minimum(k, last))
+        def _():
+            sc.finish(k)
+            sc.start(k + 1)
+
+    @pl.when(i == last)
+    def _():
+        row = jnp.sum(ngain[...], axis=0, keepdims=True)
+        width = D // total
+        which = iota((8, BLOCK), 0) == 5
+        for r in range(total):
+            piece = jnp.broadcast_to(row[:, r * width : (r + 1) * width], (8, width))
+            piece = jnp.concatenate([piece, jnp.zeros((8, BLOCK - width), F32)], axis=1)
+            packed[r] = jnp.where(which, piece, small_ref[r])
+        copies = []
+        for o in range(1, total):
+            r, dev = far(o)
+            c = pltpu.make_async_remote_copy(
+                src_ref=packed.at[r], dst_ref=smalls.at[o - 1], send_sem=ssend.at[o - 1], recv_sem=srecv.at[o - 1],
+                device_id=dev, device_id_type=MESH,
+            )
+            c.start()
+            copies.append(c)
+        sc.finish(3)
+        for c in copies:
+            c.wait()
+        acc = packed[me]
+        for o in range(1, total):
+            acc = acc + smalls[o - 1]
+        sums_ref[...] = acc
+
+
+def last_pass(ggrad, pg, tail, tok, cot, wg, wc, gain, small, gconv, T=512):
+    L = tok.shape[0]
+    n = sizes()
+    total = lax.axis_size("dp") * lax.axis_size("seq")
+    rows = D // total
+    row = lambda w: pl.BlockSpec((T, w), lambda i: (i, 0))
+    gconv = gconv.reshape(n["z"], n["x"], n["y"], n["c"], rows, WC)
+    return pl.pallas_call(
+        functools.partial(last_kernel, T),
+        grid=(L // T,),
+        in_specs=[
+            row(DI), row(WC), full((16, WC)), row(D), row(D), full((D, DI)), full((D, WC)), full((1, D)),
+            full((total, 8, BLOCK)), ANY,
+        ],
+        out_specs=[row(D), full((rows, WC)), full((8, BLOCK))],
+        out_shape=[sds((L, D), BF16), sds((rows, WC), F32), sds((8, BLOCK), F32)],
+        scratch_shapes=[
+            pltpu.VMEM((8, D), F32), pltpu.VMEM((total, 8, BLOCK), F32), pltpu.VMEM((total - 1, 8, BLOCK), F32),
+            pltpu.SemaphoreType.DMA((total - 1,)), pltpu.SemaphoreType.DMA((total - 1,)),
+        ] + scatter_scratch(rows, WC),
+        compiler_params=params(collective_id=5),
+        name="last_pass",
+    )(ggrad, pg, tail, tok, cot, wg, wc, gain, small, gconv)
+
+
 def rms_rows(tok, gain):
     x = tok.astype(F32)
     inv = lax.rsqrt(jnp.mean(x * x, axis=-1, keepdims=True) + EPS)
@@ -73,17 +611,42 @@
 
 
 def first_kernel(
-    T, tok_ref, halo_ref, wc_ref, gain_ref, conv_ref, head_ref,
-    normed_ref, convin_ref, act_ref, dt_ref, cum_ref, sig_ref, bst_ref, leave_ref, tot_ref,
-    ext, state, weighted,
+    T, tok_ref, halo_ref, wc_ref, gain_ref, conv_ref, head_ref, sg_ref, so_ref,
+    normed_ref, convin_ref, act_ref, dt_ref, cum_ref, sig_ref, bst_ref, leave_ref, tot_ref, hconv_ref, bg_ref, bo_ref,
+    ext, state, weighted, *sems,
 ):
     i = pl.program_id(0)
+    steps = pl.num_programs(0)
+    ga = Gather(sg_ref, bg_ref, "xy", sems[0:3])
+    gb = Gather(so_ref, bo_ref, "yx", sems[3:6])
 
     @pl.when(i == 0)
     def _():
+        greet(place(), "zxyc")
+        ga.start(0)
+        gb.start(0)
+
+    for stage, when in enumerate((3, 5)):
+        @pl.when(i == when)
+        def _():
+            ga.wait(stage)
+            ga.start(stage + 1)
+            gb.wait(stage)
+            gb.start(stage + 1)
+
+    @pl.when(i == steps - 1)
+    def _():
+        ga.wait(2)
+        ga.start(3)
+        gb.wait(2)
+        gb.start(3)
+
+    @pl.when(i == 0)
+    def _():
         hn = rms_rows(halo_ref[...], gain_ref[...])
-        hp = dot(hn, wc_ref[:, :CH]).astype(BF16).astype(F32)
-        ext[0:8] = hp[8:16]
+        hp = dot(hn, wc_ref[:, :CH]).astype(BF16)
+        hconv_ref[...] = hp
+        ext[0:8] = hp.astype(F32)[8:16]
         state[...] = jnp.zeros_like(state)
         tot_ref[...] = jnp.zeros_like(tot_ref)
 
@@ -133,6 +696,8 @@
     @pl.when(i == pl.num_programs(0) - 1)
     def _():
         leave_ref[...] = state[...]
+        ga.wait(3)
+        gb.wait(3)
 
 
 def sigmoid_exact(v):
@@ -140,9 +705,9 @@
 
 
 def second_kernel(
-    T, normed_ref, act_ref, dt_ref, cum_ref, bst_ref, inc_ref, tok_ref, cot_ref, wg_ref, wo_ref, row_ref, et_ref,
+    T, gate_s, act_ref, dt_ref, cum_ref, bst_ref, inc_ref, tok_ref, cot_ref, wo_ref, row_ref, et_ref,
     mixed_ref, nout_ref, ggrad_ref, mlow_ref, dcum_ref, ent_ref, egrad_ref, rg_ref, leave_ref, back_ref, cols_ref,
-    gate_s, ng, ms, growth, rlow, prod, plow, state, exg, lows,
+    ng, ms, growth, rlow, prod, plow, state, exg, lows,
 ):
     i = pl.program_id(0)
 
@@ -156,7 +721,6 @@
     lo = lane_lo()
     for c in range(DI // 256):
         cs = slice(c * 256, (c + 1) * 256)
-        gate_s[:, cs] = dot(normed_ref[...], wg_ref[:, cs]).astype(BF16)
         ng[:, cs] = dot_nt(cot_ref[...], wo_ref[cs, :])
     lower = iota((BLOCK, BLOCK), 0) >= iota((BLOCK, BLOCK), 1)
     nblk = T // BLOCK
@@ -239,12 +803,38 @@
 
 def third_kernel(
     T, act_ref, convin_ref, prev_ref, halo_ref, dt_ref, cum_ref, sig_ref, dcum_ref, mlow_ref, ent_ref, leave_ref,
-    egrad_ref, rg_ref, inc_ref, row_ref, conv_ref, head_ref, et_ref,
-    pg_ref, raw_ref, cgrad_ref, hgrad_ref, gfirst_ref, glast_ref,
-    carry, dact, vprod, prod, plow, weighted, lows, dec, nxt, gext, cext,
+    egrad_ref, rg_ref, inc_ref, row_ref, conv_ref, head_ref, et_ref, go_ref, gg_ref,
+    pg_ref, cgrad_ref, hgrad_ref, tail_ref, so_ref, sg_ref,
+    glast, gafter, hsend, hrecv, carry, dact, vprod, prod, plow, weighted, lows, dec, nxt, gext, cext, *scratch,
 ):
     i = pl.program_id(0)
     steps = pl.num_programs(0)
+    sca = Scatter(go_ref, so_ref, "yx", scratch[:NSC])
+    scb = Scatter(gg_ref, sg_ref, "xy", scratch[NSC:])
+    seq, nseq = lax.axis_index("seq"), lax.axis_size("seq")
+    after = pltpu.make_async_remote_copy(
+        src_ref=gext.at[0:8], dst_ref=gafter, send_sem=hsend, recv_sem=hrecv, device_id={"seq": seq - 1},
+        device_id_type=MESH,
+    )
+
+    @pl.when(i == 0)
+    def _():
+        greet(place(), "zxyc", 1)
+        sca.start(0)
+        scb.start(0)
+
+    for stage, when in enumerate((1, 4, 6)):
+        @pl.when(i == when)
+        def _():
+            sca.finish(stage)
+            sca.start(stage + 1)
+            scb.finish(stage)
+            scb.start(stage + 1)
+
+    @pl.when(i == steps - 1)
+    def _():
+        sca.finish(3)
+        scb.finish(3)
 
     @pl.when(i == 0)
     def _():
@@ -321,7 +911,7 @@
         dc = dcum_ref[rows] - used + jnp.where(last, de, 0.0)
         da_log = dot_exact(triu, dc)
         draw = (c + da_log * head_ref[1:2]) * sig_ref[rows]
-        raw_ref[rows] = draw.astype(BF16)
+        pg_ref[rows, CH:] = draw.astype(BF16)
         hgrad_ref[0:8] += jnp.sum(draw.reshape(16, 8, BLOCK), axis=0)
         hgrad_ref[8:16] += jnp.sum((da_log * dt).reshape(16, 8, BLOCK), axis=0) * head_ref[1:2]
         nxt[...] = ent_ref[blk]
@@ -349,19 +939,47 @@
 
         @pl.when(i == 0)
         def _():
-            glast_ref[:, cs] = back[T - 8 :]
+            glast[:, cs] = back[T - 16 :]
+            pg_ref[T - 16 :, cs] = jnp.zeros((16, 128), BF16)
 
     @pl.when(i == steps - 1)
     def _():
-        gfirst_ref[...] = gext[0:8]
+        @pl.when(seq > 0)
+        def _():
+            after.start()
+
+        @pl.when(seq == nseq - 1)
+        def _():
+            gafter[...] = jnp.zeros_like(gafter)
+
+        @pl.when(seq < nseq - 1)
+        def _():
+            after.wait_recv()
+
+        rows16 = iota((16, CH), 0)
+        tail = glast[...]
+        for i3 in range(CONV - 1):
+            fix = jnp.zeros((1, CH), F32)
+            for k in range(i3 + 1):
+                fix = fix + conv_ref[k : k + 1] * gafter[i3 - k : i3 - k + 1]
+            tail = tail + jnp.where(rows16 == 13 + i3, fix, 0.0)
+        tail_ref[:, :CH] = tail.astype(BF16)
+        tail_ref[:, CH:] = jnp.zeros((16, BLOCK), BF16)
+
+        @pl.when(seq > 0)
+        def _():
+            after.wait_send()
 
 
 def full(shape):
     return pl.BlockSpec(shape, lambda i: (0,) * len(shape))
 
 
-def params():
-    return pltpu.CompilerParams(dimension_semantics=("arbitrary",), vmem_limit_bytes=VMEM_LIMIT)
+def params(collective_id=None):
+    return pltpu.CompilerParams(
+        dimension_semantics=("arbitrary",), vmem_limit_bytes=VMEM_LIMIT, collective_id=collective_id,
+        has_side_effects=collective_id is not None,
+    )
 
 
 def head_columns():
@@ -374,31 +992,37 @@
     return jax.ShapeDtypeStruct(shape, dtype)
 
 
-def first_pass(tok, halo, wc, gain, conv, head, T=256):
+def first_pass(tok, halo, wc, gain, conv, head, slab_g, slab_o, T=256):
     L = tok.shape[0]
     nb, per = L // BLOCK, T // BLOCK
+    n = sizes()
     row = lambda w: pl.BlockSpec((T, w), lambda i: (i, 0))
+    dims = (n["z"], n["x"], n["y"], n["c"])
     return pl.pallas_call(
         functools.partial(first_kernel, T),
         grid=(L // T,),
-        in_specs=[row(D), full((16, D)), full((D, CH + BLOCK)), full((1, D)), full((8, CH)), full((8, BLOCK))],
+        in_specs=[
+            row(D), full((16, D)), full((D, WC)), full((1, D)), full((8, CH)), full((8, BLOCK)), ANY, ANY,
+        ],
         out_specs=[
             row(D), row(CH), row(CH), row(BLOCK), row(BLOCK), row(BLOCK),
             pl.BlockSpec((per, NSTATE, DI), lambda i: (i, 0, 0)), full((NSTATE, DI)), full((8, BLOCK)),
+            full((16, CH)), ANY, ANY,
         ],
         out_shape=[
             sds((L, D), BF16), sds((L, CH), BF16), sds((L, CH), BF16), sds((L, BLOCK), F32), sds((L, BLOCK), F32),
             sds((L, BLOCK), F32), sds((nb, NSTATE, DI), BF16), sds((NSTATE, DI), F32), sds((8, BLOCK), F32),
+            sds((16, CH), BF16), sds(dims + slab_g.shape, BF16), sds(dims + slab_o.shape, BF16),
         ],
         scratch_shapes=[
             pltpu.VMEM((T + 8, CH), F32), pltpu.VMEM((NSTATE, DI), F32), pltpu.VMEM((BLOCK, DI), BF16),
-        ],
-        compiler_params=params(),
+        ] + gather_sems() + gather_sems(),
+        compiler_params=params(collective_id=1),
         name="first_pass",
-    )(tok, halo, wc, gain, conv, head)
-
-
-def second_pass(normed, act, dt, cum, bst, inc, tok, cot, wg, wo, rows, et, T=256):
+    )(tok, halo, wc, gain, conv, head, slab_g, slab_o)
+
+
+def second_pass(gate, act, dt, cum, bst, inc, tok, cot, wo, rows, et, T=256):
     L = tok.shape[0]
     nb, per = L // BLOCK, T // BLOCK
     row = lambda w: pl.BlockSpec((T, w), lambda i: (i, 0))
@@ -407,7 +1031,7 @@
         functools.partial(second_kernel, T),
         grid=(L // T,),
         in_specs=[
-            row(D), row(CH), row(BLOCK), row(BLOCK), blk, full((NSTATE, DI)), row(D), row(D), full((D, DI)),
+            row(DI), row(CH), row(BLOCK), row(BLOCK), blk, full((NSTATE, DI)), row(D), row(D),
             full((DI, D)), full((8, DI)), full((DI, BLOCK)),
         ],
         out_specs=[
@@ -420,17 +1044,25 @@
             sds((NSTATE, DI), F32), sds((16, DI), F32),
         ],
         scratch_shapes=[
-            pltpu.VMEM((T, DI), BF16), pltpu.VMEM((T, DI), F32), pltpu.VMEM((T, DI), F32), pltpu.VMEM((T, DI), F32),
+            pltpu.VMEM((T, DI), F32), pltpu.VMEM((T, DI), F32), pltpu.VMEM((T, DI), F32),
             pltpu.VMEM((T, DI), BF16), pltpu.VMEM((T, DI), BF16), pltpu.VMEM((T, DI), BF16), pltpu.VMEM((NSTATE, DI), F32),
             pltpu.VMEM((8, DI), F32), pltpu.VMEM((per, NSTATE, DI), BF16),
         ],
         compiler_params=params(),
         name="second_pass",
-    )(normed, act, dt, cum, bst, inc, tok, cot, wg, wo, rows, et)
-
-
-def third_pass(act, convin, halo, dt, cum, sig, dcum, mlow, ent, leave, egrad, rg, inc, rows, conv, head, et, T=256):
+    )(gate, act, dt, cum, bst, inc, tok, cot, wo, rows, et)
+
+
+def third_pass(
+    act, convin, halo, dt, cum, sig, dcum, mlow, ent, leave, egrad, rg, inc, rows, conv, head, et, go, gg, T=256
+):
     L = act.shape[0]
+    m = sizes()
+    dims = (m["z"], m["x"], m["y"], m["c"])
+    total = m["z"] * m["y"] * 4
+    ro, rg_rows = DI // total, D // total
+    go = go.reshape(dims + (ro, D))
+    gg = gg.reshape(dims + (rg_rows, DI))
     n, per = L // T, T // BLOCK
     row = lambda w: pl.BlockSpec((T, w), lambda i: (n - 1 - i, 0))
     blk = pl.BlockSpec((per, NSTATE, DI), lambda i: (n - 1 - i, 0, 0))
@@ -441,101 +1073,90 @@
         in_specs=[
             row(CH), row(CH), prev, full((16, CH)), row(BLOCK), row(BLOCK), row(BLOCK), row(BLOCK), row(DI), blk,
             full((NSTATE, DI)), blk, row(BLOCK), full((NSTATE, DI)), full((8, DI)), full((8, CH)), full((8, BLOCK)),
-            full((DI, BLOCK)),
-        ],
-        out_specs=[row(CH), row(BLOCK), full((40, CH)), full((16, BLOCK)), full((8, CH)), full((8, CH))],
+            full((DI, BLOCK)), ANY, ANY,
+        ],
+        out_specs=[
+            row(WC), full((40, CH)), full((16, BLOCK)), full((16, WC)), full((ro, D)), full((rg_rows, DI)),
+        ],
         out_shape=[
-            sds((L, CH), BF16), sds((L, BLOCK), BF16), sds((40, CH), F32), sds((16, BLOCK), F32), sds((8, CH), F32),
-            sds((8, CH), F32),
+            sds((L, WC), BF16), sds((40, CH), F32), sds((16, BLOCK), F32), sds((16, WC), BF16), sds((ro, D), F32),
+            sds((rg_rows, DI), F32),
         ],
         scratch_shapes=[
+            pltpu.VMEM((16, CH), F32), pltpu.VMEM((8, CH), F32), pltpu.SemaphoreType.DMA(()), pltpu.SemaphoreType.DMA(()),
             pltpu.VMEM((NSTATE, DI), F32), pltpu.VMEM((T, CH), F32), pltpu.VMEM((BLOCK, DI), BF16), pltpu.VMEM((BLOCK, DI), BF16), pltpu.VMEM((BLOCK, DI), BF16),
             pltpu.VMEM((BLOCK, DI), BF16), pltpu.VMEM((NSTATE, DI), BF16), pltpu.VMEM((8, DI), F32),
             pltpu.VMEM((NSTATE, DI), BF16), pltpu.VMEM((T + 8, CH), F32), pltpu.VMEM((T + 16, CH), F32),
-        ],
-        compiler_params=params(),
+        ] + scatter_scratch(ro, D) + scatter_scratch(rg_rows, DI),
+        compiler_params=params(collective_id=4),
         name="third_pass",
-    )(act, convin, convin, halo, dt, cum, sig, dcum, mlow, ent, leave, egrad, rg, inc, rows, conv, head, et)
-
-
-def from_behind(x, axis, by):
-    peers = lax.axis_size(axis)
-    pairs = [(i, i + by) for i in range(peers) if 0 <= i + by < peers]
-    return lax.ppermute(x, axis, pairs)
-
-
-def chain(total, leaving, axis, reverse):
-    peers, index = lax.axis_size(axis), lax.axis_index(axis)
-    decays = lax.all_gather(total, axis)
-    states = lax.all_gather(leaving.astype(BF16), axis)
-    acc = jnp.zeros(leaving.shape, F32)
-    for k in range(peers):
-        at = peers - 1 - k if reverse else k
-        reached = (at > index) if reverse else (at < index)
-        acc = jnp.where(reached, acc * decays[at] + states[at].astype(F32), acc)
-    return acc
+    )(act, convin, convin, halo, dt, cum, sig, dcum, mlow, ent, leave, egrad, rg, inc, rows, conv, head, et, go, gg)
 
 
 def pad_lanes(x, width):
     return jnp.pad(x, ((0, 0), (0, width - x.shape[1])))
+
+
+def pad_block(x, rows, lanes):
+    return jnp.pad(x, ((0, rows - x.shape[0]), (0, lanes - x.shape[1])))
 
 
 def on_device(
     tokens, cotangent, norm_gain, in_weight, conv_weight, conv_bias, step_bias, decay_log, skip_gain, gate_gain,
     out_weight,
 ):
-    both = ("dp", "seq")
-    gather = functools.partial(lax.all_gather, axis_name=both, axis=0, tiled=True)
-    w_in = gather(in_weight)
-    wo = gather(out_weight)
-    taps = gather(conv_weight)
-    small = gather(norm_gain), gather(conv_bias), gather(gate_gain)
     tok, cot = tokens[0], cotangent[0]
     L = tok.shape[0]
-    wg = w_in[:, :DI]
-    wc = jnp.pad(w_in[:, DI:], ((0, 0), (0, DI + CH + BLOCK - w_in.shape[1])))
-    gain = small[0].astype(F32)[None]
-    conv = jnp.concatenate([taps.astype(F32).T, small[1].astype(F32)[None], jnp.zeros((3, CH), F32)], axis=0)
+    k_rows, c_rows, g_rows = in_weight.shape[0], conv_weight.shape[0], gate_gain.shape[0]
+    spare = BLOCK - HEADS
+    last_row = jnp.concatenate([norm_gain, gate_gain])[None]
+    extra = jnp.concatenate(
+        [pad_lanes(conv_weight.T, spare), pad_lanes(conv_bias[None], spare), pad_lanes(last_row, spare)], axis=0
+    )
+    slab_c = jnp.concatenate([in_weight[:, DI:], pad_block(extra, k_rows, spare)], axis=1)
+    buf, halo = gather_weights(slab_c, tok[L - 16 :])
+    total = D // k_rows
+    wc = buf.reshape(D, WC)
+    spread = buf.reshape(total, k_rows, WC)[:, :6, CH + HEADS :].astype(F32)
+    conv = jnp.swapaxes(spread[:, :5, :c_rows], 0, 1).reshape(5, total * c_rows)
+    conv = jnp.pad(conv, ((0, 3), (0, 0)))
+    gain = spread[:, 5, :k_rows].reshape(1, D)
+    ggain = spread[:, 5, k_rows : k_rows + g_rows].reshape(1, DI)
     head = pad_lanes(jnp.stack([step_bias, -jnp.exp(decay_log)] + [jnp.zeros_like(step_bias)] * 6), BLOCK)
     skip = jnp.repeat(skip_gain, HEADDIM)[None]
-    rows = jnp.concatenate([small[2].astype(F32)[None], skip, jnp.zeros((6, DI), F32)], axis=0)
+    rows = jnp.concatenate([ggain, skip, jnp.zeros((6, DI), F32)], axis=0)
     et = jnp.asarray(head_columns(), BF16)
 
-    halo = from_behind(tok[L - 16 :], "seq", 1)
-    normed, convin, act, dt, cum, sig, bst, leave, tot = first_pass(tok, halo, wc, gain, conv, head)
-    total = jnp.repeat(jnp.exp2(tot[0, :HEADS]), HEADDIM)[None]
-    inc = chain(total, leave, "seq", False)
+    normed, convin, act, dt, cum, sig, bst, leave, tot, hconv, buf_g, buf_o = first_pass(
+        tok, halo, wc, gain, conv, head, in_weight[:, :DI], out_weight
+    )
+    wg, wo = buf_g.reshape(D, DI), buf_o.reshape(DI, D)
+    gate, inc = gate_pass(normed, wg, leave, tot)
     mixed, nout, ggrad, mlow, dcum, ent, egrad, rg, leave2, back, cols = second_pass(
-        normed, act, dt, cum, bst, inc, tok, cot, wg, wo, rows, et
+        gate, act, dt, cum, bst, inc, tok, cot, wo, rows, et
     )
-    g_out = lax.dot_general(nout, cot, (((0,), (0,)), ((), ())), preferred_element_type=F32)
-    g_gate = lax.dot_general(normed, ggrad, (((0,), (0,)), ((), ())), preferred_element_type=F32)
-    later = chain(total, back, "seq", True)
-    halo_conv = from_behind(convin[L - 16 :], "seq", 1)
-    pg, raw, cgrad, hgrad, gfirst, glast = third_pass(
-        act, convin, halo_conv, dt, cum, sig, dcum, mlow, ent, leave2, egrad, rg, later, rows, conv, head, et
+    g_out, g_gate, later = grads_pass(nout, cot, normed, ggrad, back, tot)
+    pg, cgrad, hgrad, tail, out_grad, gate_cols = third_pass(
+        act, convin, hconv, dt, cum, sig, dcum, mlow, ent, leave2, egrad, rg, later, rows, conv, head, et, g_out, g_gate
     )
-    after = from_behind(gfirst, "seq", -1)
-    fix = [sum(conv[k] * after[i - k] for k in range(i + 1)) for i in range(CONV - 1)]
-    tail = glast[5:8] + jnp.stack(fix)
-    pg = lax.dynamic_update_slice(pg, tail.astype(BF16), (L - 3, 0))
-    g_conv = lax.dot_general(normed, pg, (((0,), (0,)), ((), ())), preferred_element_type=F32)
-    g_step = lax.dot_general(normed, raw, (((0,), (0,)), ((), ())), preferred_element_type=F32)
-    nig = dot_nt(ggrad, wg) + dot_nt(pg, wc[:, :CH]) + dot_nt(raw, wc[:, CH:])
-    x = tok.astype(F32)
-    inv = lax.rsqrt(jnp.mean(x * x, axis=-1, keepdims=True) + EPS)
-    u = nig * gain
-    tgrad = (cot.astype(F32) + inv * u - x * (inv**3 * jnp.mean(u * x, axis=-1, keepdims=True))).astype(BF16)
-    norm_gain_grad = jnp.sum(nig * x * inv, axis=0)
-    in_grad = jnp.concatenate([g_gate, g_conv, g_step[:, :HEADS]], axis=1)
+    g_conv = conv_grad(normed, pg, tail)
     cg = cgrad.reshape(5, 8, CH).sum(axis=1)
-    scatter = functools.partial(lax.psum_scatter, axis_name=both, scatter_dimension=0, tiled=True)
     hg = hgrad.reshape(2, 8, BLOCK).sum(axis=1)[:, :HEADS]
     gg = cols.reshape(2, 8, DI).sum(axis=1)
-    sums = lax.psum((hg[0], hg[1], gg[1].reshape(HEADS, HEADDIM).sum(axis=1)), both)
+    sums = jnp.concatenate([hg[0], hg[1], gg[1].reshape(HEADS, HEADDIM).sum(axis=1)])
+    lanes = lambda x: jnp.pad(x, ((0, 0),) * (x.ndim - 1) + ((0, BLOCK - x.shape[-1]),))
+    small = jnp.concatenate(
+        [
+            lanes(jnp.swapaxes(cg.reshape(5, total, c_rows), 0, 1)), jnp.zeros((total, 1, BLOCK), F32),
+            lanes(gg[0].reshape(total, 1, g_rows)), jnp.broadcast_to(lanes(sums[None, None]), (total, 1, BLOCK)),
+        ],
+        axis=1,
+    )
+    tgrad, conv_cols, out = last_pass(ggrad, pg, tail, tok, cot, wg, wc, gain, small, g_conv)
+    in_grad = jnp.concatenate([gate_cols, conv_cols[:, : CH + HEADS]], axis=1)
     return (
-        mixed[None], tgrad[None], scatter(norm_gain_grad), scatter(in_grad), scatter(cg[:4].T), scatter(cg[4]),
-        sums[0], sums[1], sums[2], scatter(gg[0]), scatter(g_out),
+        mixed[None], tgrad[None], out[5, :k_rows], in_grad, out[:4, :c_rows].T, out[4, :c_rows],
+        out[7, :HEADS], out[7, HEADS : 2 * HEADS], out[7, 2 * HEADS : 3 * HEADS], out[6, :g_rows], out_grad,
     )
 
 

time: 573 us -> 355 us (0.62)
  Pallas kernels: 169 us -> 329 us
  waiting for transfers between devices: 145 us -> 0 us
  blocking collectives: 129 us -> 0 us
  matrix products: 53.5 us -> 0 us
  other arithmetic: 27.3 us -> 7.01 us
  between operations: 14.9 us -> 0.85 us
  starting transfers between devices: 6.03 us -> 0 us
    pallas_call x0 -> x5, Pallas kernels: none -> 139 us  [the longest x1 54.9 us: last_pass(): pl.pallas_call(functools.partial(last_kernel, T), grid=(L // T,), in_spec...]
    unnamed x2 -> x0, blocking collectives: 83.1 us -> none
    unnamed x7 -> x0, waiting for transfers between devices: 81.9 us -> none
    all_gather x4 -> x0, waiting for transfers between devices: 62.1 us -> none  [the longest x1 57.5 us: on_device(): wo = gather(out_weight)]
    dot_general x7 -> x0, matrix products: 53.5 us -> none  [the longest x3 21.5 us: dot_nt(): return lax.dot_general(a, b, NT, preferred_element_type=F32)]
    all_gather x2 -> x0, blocking collectives: 46.1 us -> none  [the longest x1 40.6 us: on_device(): taps = gather(conv_weight)]
    pallas_call x1, Pallas kernels: 76.2 us -> 87.9 us  [third_pass(): pl.pallas_call(functools.partial(third_kernel, T), grid=(n,), in_specs=[r...]
    pallas_call x1, Pallas kernels: 35.6 us -> 46.7 us  [first_pass(): pl.pallas_call(functools.partial(first_kernel, T), grid=(L // T,), in_spe...]
  transfers between devices with their start and end apart: 9 -> 0, of which waited for: 4 -> 0; matrix products, arithmetic and copies ran while one was open for 17% -> 0% of each run, Pallas kernels for 13% -> 0%
where the time goes in v2:
time: 355 us; the launch traced here: 354 us
  Pallas kernels  329 us (93%)
  local copies, waits for them, and re-layouts  17.3 us (5%)
  other arithmetic  7.01 us (2%)
    pallas_call x1, Pallas kernels, third_pass(): pl.pallas_call(functools.partial(third_kernel, T), grid=(n,), in_specs=[r...  87.9 us
    pallas_call x1, Pallas kernels, second_pass(): pl.pallas_call(functools.partial(second_kernel, T), grid=(L // T,), in_sp...  55.8 us
    pallas_call x1, Pallas kernels, last_pass(): pl.pallas_call(functools.partial(last_kernel, T), grid=(L // T,), in_spec...  54.9 us
    pallas_call x1, Pallas kernels, first_pass(): pl.pallas_call(functools.partial(first_kernel, T), grid=(L // T,), in_spe...  46.7 us
    pallas_call x1, Pallas kernels, gather_weights(): pl.pallas_call(weights_kernel, in_specs=[ANY, vm], out_specs=[ANY, vm], o...  31.4 us
    pallas_call x1, Pallas kernels, grads_pass(): pl.pallas_call(grads_kernel, grid=(6,), in_specs=[col(256), full((L, D)),...  27.8 us
    pallas_call x1, Pallas kernels, conv_grad(): pl.pallas_call(conv_grad_kernel, grid=(3,), in_specs=[pl.BlockSpec((L, 25...  14.5 us
    pallas_call x1, Pallas kernels, gate_pass(): pl.pallas_call(gate_kernel, grid=(L // T,), in_specs=[row(D), full((D, DI...  9.89 us

profile of v2, /device:TPU:0, one launch (start us, length us, event | category | flops | bytes accessed | tf_op | source)
XLA Modules:
  0.0 354.0 jit_solution(13536578733706111822)
XLA Ops:
  0.6 0.9 slice.63
  1.5 0.7 maximum_bitcast_fusion
  2.3 0.7 fusion.9
  3.0 0.7 fusion.3.slab
  3.7 1.3 slice_bitcast_fusion.1.last
  5.1 31.4 %gather_weights.1 = (bf16[4,2,2,2,24,1920]{5,4,3,2,1,0:T(8,128)(2,1)}, bf16[16,768]{1,0:T(8,128)(2,1)}) custom-call(bf16[24,1920]{1,0:T(8,128)(2,1)} %fusion.3.slab, bf16[16,768]{1,0:T(8,128)(2,1)} %slice_bitcast_fusion.1.last), custom_call_target="tpu_custom_call" | custom-call | tf_op jit(solution)/shard_map/gather_weights/pallas_call | solution.py:394
  36.5 0.9 slice.83
  37.4 0.1 reshape.63
  37.5 0.6 pad.40.conv_ref
  38.2 0.7 reshape_squeeze.12.gain_ref
  38.9 0.1 pad.59.clone
  38.9 0.1 pad.60.clone
  39.0 0.7 negate_bitcast_fusion
  39.7 0.7 maximum_maximum_fusion.1
  40.4 0.6 pad.41.head_ref
  41.0 1.5 slice.69.sg_ref
  42.5 46.7 %first_pass.1 = (bf16[2048,768]{1,0:T(8,128)(2,1)}, bf16[2048,1792]{1,0:T(8,128)(2,1)}, bf16[2048,1792]{1,0:T(8,128)(2,1)}, f32[2048,128]{1,0:T(8,128)}, f32[204...) custom-call(bf16[2048,768]{1,0:T(8,128)(2,1)} %bitcast.59, ...), custom_call_target="tpu_custom_call" | custom-call | tf_op jit(solution)/shard_map/first_pass/pallas_call | solution.py:1001
  89.2 0.0 copy-start.5
  89.2 9.9 %gate_pass.1 = (bf16[2048,1536]{1,0:T(8,128)(2,1)}, f32[128,1536]{1,0:T(8,128)}) custom-call(bf16[2048,768]{1,0:T(8,128)(2,1)} %get-tuple-element.52.normed_ref.tnormed_ref, bf16[768,1536]{1,0:T(8,128)(2,1)} %bitcast.69, f32[128,1536]{1,0:T(8,128)} %get-tuple-element.54.leave_ref, f32[8,128]{1,0:T(8,128)} %get-tuple-element.55.tot_ref), custom_call_target="tpu_custom_call" | custom-call | tf_op jit(solution)/shard_map/gate_pass/pallas_call | solution.py:432
  99.1 0.1 slice.86
  99.2 0.1 reshape_squeeze.13
  99.3 0.1 broadcast_in_dim.33
  99.4 0.1 broadcast_in_dim_reshape.3
  99.5 0.1 pad.56.clone
  99.5 0.7 maximum_maximum_fusion.row_ref
  100.2 55.8 %second_pass.1 = (bf16[2048,768]{1,0:T(8,128)(2,1)}, bf16[2048,1536]{1,0:T(8,128)(2,1)}, bf16[2048,1536]{1,0:T(8,128)(2,1)}, bf16[2048,1536]{1,0:T(8,128)(2,1)},...) custom-call(bf16[2048,1536]{1,0:T(8,128)(2,1)} %get-tuple-element.56, ...), custom_call_target="tpu_custom_call" | custom-call | tf_op jit(solution)/shard_map/second_pass/pallas_call | solution.py:1030
  156.0 27.8 %grads_pass.1 = (bf16[1536,768]{1,0:T(8,128)(2,1)}, bf16[768,1536]{1,0:T(8,128)(2,1)}, f32[128,1536]{1,0:T(8,128)}) custom-call(bf16[2048,1536]{1,0:T(8,128)(2,1)} %get-tuple-element.74.nout_ref, bf16[2048,768]{1,0:T(8,128)(2,1)} %bitcast.63, bf16[2048,768]{1,0:T(8,128)(2,1)} %get-tuple-element.52.normed_ref.tnormed_ref, ...), custom_call_target="tpu_custom_call" | custom-call | tf_op jit(solution)/shard_map/grads_pass/pallas_call | solution.py:470
  183.8 87.9 %third_pass.1 = (bf16[2048,1920]{1,0:T(8,128)(2,1)}, f32[40,1792]{1,0:T(8,128)}, f32[16,128]{1,0:T(8,128)}, bf16[16,1920]{1,0:T(8,128)(2,1)}, f32[48,768]{1,0:T(8,128)}, /*index=5*/f32[24,1536]{1,0:T(8,128)}) custom-call(bf16[2048,1792]{1,0:T(8,128)(2,1)} %get-tuple-element.57.act_ref, bf16[2048,1792]{1,0:T(8,128)(2,1)} %get-tuple-element.65.convin_ref.prev_ref, ...), custom_call_target="tpu_custom_call" | custom-call | tf_op jit(solution)/shard_map/third_pass/pallas_call | solution.py:1070
  271.8 0.0 copy-start.3
  271.8 0.0 copy-start
  271.8 14.5 %conv_grad.1 = bf16[768,1920]{1,0:T(8,128)(2,1)} custom-call(bf16[2048,768]{1,0:T(8,128)(2,1)} %get-tuple-element.52.normed_ref.tnormed_ref, bf16[2048,1920]{1,0:T(8,128)(2,1)} %get-tuple-element.79.pg_ref, bf16[2048,768]{1,0:T(8,128)(2,1)} %get-tuple-element.52.normed_ref.tnormed_ref, bf16[16,1920]{1,0:T(8,128)(2,1)} %get-tuple-element.80.tail_ref), custom_call_target="tpu_custom_call" | custom-call | tf_op jit(solution)/shard_map/conv_grad/pallas_call | solution.py:493
  286.4 0.1 reshape_squeeze.15
  286.5 0.1 reduce_sum.39
  286.6 0.1 maximum_bitcast_fusion.1
  286.7 0.1 bitcast_reduce_fusion
  286.8 0.1 reshape.69
  286.9 0.1 copy.29
  287.0 0.1 reshape_squeeze.14
  287.1 0.1 pad.48.clone
  287.2 0.7 fusion.1.small_ref
  287.9 54.9 %last_pass.1 = (bf16[2048,768]{1,0:T(8,128)(2,1)}, f32[24,1920]{1,0:T(8,128)}, f32[8,128]{1,0:T(8,128)}) custom-call(bf16[2048,1536]{1,0:T(8,128)(2,1)} %get-tuple-element.64.ggrad_ref, bf16[2048,1920]{1,0:T(8,128)(2,1)} %get-tuple-element.79.pg_ref, bf16[16,1920]{1,0:T(8,128)(2,1)} %get-tuple-element.80.tail_ref, bf16[2048,768]{1,0:T(8,128)(2,1)} %bitcast.61, ...), custom_call_target="tpu_custom_call" | custom-call | tf_op jit(solution)/shard_map/last_pass/pallas_call | solution.py:589
  342.8 1.7 pad_maximum_fusion
  344.5 1.4 slice_bitcast_fusion.4
  345.9 1.3 slice_bitcast_fusion.2
  347.2 1.2 slice_bitcast_fusion.3
  348.4 1.2 slice_bitcast_fusion.7
  349.6 3.8 %copy.32 = bf16[1,2048,768]{2,1,0:T(8,128)(2,1)} copy(bf16[1,2048,768]{2,1,0:T(8,128)(2,1)} %bitcast.71) | data formatting | bytes 6291456
  353.4 0.7 copy.33
  (21 shorter events, 0.2 us)
Async XLA Ops:
  89.2 10.1 %copy-start.5 = (f32[24]{0:T(128)S(1)}, f32[24]{0:T(128)}, u32[]{:S(2)}) copy-start(f32[24]{0:T(128)} %param.20) | copy-start | bytes 292
  271.8 14.5 %copy-start.4 = (f32[16,128]{1,0:T(8,128)S(1)}, f32[16,128]{1,0:T(8,128)}, u32[]{:S(2)}) copy-start(f32[16,128]{1,0:T(8,128)} %get-tuple-element.83) | copy-start | bytes 24580
  271.8 14.6 %copy-start.3 = (f32[16,1536]{1,0:T(8,128)S(1)}, f32[16,1536]{1,0:T(8,128)}, u32[]{:S(2)}) copy-start(f32[16,1536]{1,0:T(8,128)} %get-tuple-element.82) | copy-start | bytes 294916
  271.8 14.9 %copy-start = (f32[40,1792]{1,0:T(8,128)S(1)}, f32[40,1792]{1,0:T(8,128)}, u32[]{:S(2)}) copy-start(f32[40,1792]{1,0:T(8,128)} %get-tuple-element.81) | copy-start | bytes 860164
  287.9 54.9 %copy-start.2 = (f32[24,1536]{1,0:T(8,128)S(1)}, f32[24,1536]{1,0:T(8,128)}, u32[]{:S(2)}) copy-start(f32[24,1536]{1,0:T(8,128)} %get-tuple-element.86) | copy-start | bytes 442372
  349.6 3.8 %copy-start.1 = (f32[48,768]{1,0:T(8,128)S(1)}, f32[48,768]{1,0:T(8,128)}, u32[]{:S(2)}) copy-start(f32[48,768]{1,0:T(8,128)} %get-tuple-element.118) | copy-start | bytes 442372
